TPU v7x, 128 devices: a whole 4x4x4 slice. The times are simulated.
128 devices in a mesh: atoms: 32 (over y, x, core), kvec: 4 (over z).
Axes of the slice: x: 4, y: 4, z: 4, core: 2. Of those that a mesh axis runs over, the one named last changes fastest.
Arguments:
- positions: float32 [3, 16384], P(None, 'atoms'), as said below
- features: float32 [64, 16384], P(None, 'atoms'), may hold values from -6 to 6
- filter_one: float32 [16, 64], replicated, may hold values from -0.75 to 0.75
- filter_two: float32 [16, 64], replicated, may hold values from -0.75 to 0.75
- readout_in: float32 [64, 64], replicated, may hold values from -0.75 to 0.75
- readout_out: float32 [64], replicated, may hold values from -0.75 to 0.75
- charge_weight: float32 [64, 16], replicated, may hold values from -0.75 to 0.75
- neighbour_blocks: int32 [128, 9], P('atoms'), may hold values from 0 to 127, as said below
- live_slots: int32 [128], P('atoms'), may hold values from 4 to 9
- wave_ints: int32 [3, 8192], P(None, 'kvec'), may hold values from -16 to 56, as said below
Outputs:
- forces: float32 [3, 16384], P(None, 'atoms')
Inputs may be any that keep to these rules, and one draw needn't show every extreme that they name: `neighbour_blocks`: slot 0 of row b is b; slots 1 to live_slots[b] - 1 list different blocks other than b, each on the same index of atoms as b or on one next to it, blocks being numbered 4 to an index in order; the remaining slots repeat b. `positions`: atoms of index p of atoms lie in x between 5 p and 5 p + 5 and in y between 0 and 10; the atoms of one block lie within a z range of length 128 / 5. `wave_ints`: the 8192 triples are different and nonzero; each has a positive first entry, or a zero first entry and a positive second, or zero first and second entries and a positive third; the second entry lies within -4 and 4.
All inputs are finite; a program needn't handle non-finite values.
Results may differ from a plain program's by a relative error of at most 0.0003.
Values sent between devices are 32-bit elements; how exact they have to be, the bound alone decides.
A program may use at most 64 MiB of HBM per device.

v0:
```python
import math

import jax
import jax.numpy as jnp
from jax import lax
from jax.sharding import PartitionSpec as P

highest = lax.Precision.HIGHEST
slab_width = 5.0
slab_height = 10.0
atom_density = 0.1
cutoff_radius = 5.0
self_offset = 0.0001
screen_square = 0.25
spread_square = 1.0


def padded(shard, sides, width):
    for axis, dim in sides:
        count, length = (lax.axis_size(axis), shard.shape[dim])
        up = [(i, (i + 1) % count) for i in range(count - 1)]
        down = [(j, i) for i, j in up]
        last = lax.slice_in_dim(shard, length - width, length, axis=dim)
        first = lax.slice_in_dim(shard, 0, width, axis=dim)
        before = lax.ppermute(last, axis, up)
        after = lax.ppermute(first, axis, down)
        shard = jnp.concatenate([before, shard, after], axis=dim)
    return shard


def from_behind(block, axis, distance):
    devices = range(lax.axis_size(axis))
    route = [(i - distance, i) for i in devices if i - distance in devices]
    return lax.ppermute(block, axis, route)


def radial(distance, basis_count):
    steps_along = jnp.arange(basis_count).astype(jnp.float32)
    centers = cutoff_radius * steps_along / (basis_count - 1)
    sharpness = 0.5 * ((basis_count - 1) / cutoff_radius) ** 2
    envelope = jnp.where(
        distance < cutoff_radius, 0.5 * (jnp.cos(jnp.pi * distance / cutoff_radius) + 1.0), 0.0
    )
    shaped = centers.reshape((basis_count,) + (1,) * distance.ndim)
    return envelope[None] * jnp.exp(-sharpness * (distance[None] - shaped) ** 2)


def block_messages(centre, near_pos, near_val, live_row, filter_pair):
    block_size = centre.shape[1]
    slot_count = near_pos.shape[1]
    basis_count = filter_pair.shape[0]
    offset = centre[:, :, None, None] - near_pos[:, None, :, :]
    distance = jnp.sqrt(jnp.sum(offset * offset, axis=0) + self_offset)
    atom_left = jnp.arange(block_size)[:, None, None]
    atom_right = jnp.arange(block_size)[None, None, :]
    slot_number = jnp.arange(slot_count)[None, :, None]
    active = live_row[None, :, None] & ((slot_number > 0) | (atom_left != atom_right))
    radial_terms = radial(distance, basis_count) * active[None].astype(distance.dtype)
    radial_terms = radial_terms.reshape(basis_count, block_size, slot_count * block_size)
    values = near_val.reshape(near_val.shape[0], slot_count * block_size)
    gathered = jnp.einsum("mij,fj->mfi", radial_terms, values, precision=highest)
    return jnp.einsum("mf,mfi->fi", filter_pair, gathered, precision=highest)


def messages(own_pos, wide_pos, wide_values, filter_pair, near_ids, live_mask, block_size):
    block_count = near_ids.shape[0]
    own_blocks = own_pos.reshape(3, block_count, block_size)
    pos_blocks = wide_pos.reshape(3, -1, block_size)
    value_blocks = wide_values.reshape(wide_values.shape[0], -1, block_size)

    def per_block(block_index):
        chosen = near_ids[block_index]
        centre = lax.dynamic_index_in_dim(own_blocks, block_index, 1, keepdims=False)
        near_pos = jnp.take(pos_blocks, chosen, axis=1)
        near_val = jnp.take(value_blocks, chosen, axis=1)
        return block_messages(centre, near_pos, near_val, live_mask[block_index], filter_pair)

    result = lax.map(jax.checkpoint(per_block), jnp.arange(block_count, dtype=jnp.int32))
    return jnp.transpose(result, (1, 0, 2)).reshape(wide_values.shape[0], -1)


def widen_rows(values):
    local_atoms = values.shape[1]
    return padded(values, (("atoms", 1),), local_atoms)


def send_back(widened):
    local_atoms = widened.shape[1] // 3
    summed = widened[:, local_atoms : 2 * local_atoms]
    for step_by, piece in ((-1, widened[:, :local_atoms]), (1, widened[:, 2 * local_atoms :])):
        summed = summed + from_behind(piece, "atoms", step_by)
    return summed


def body(
    positions,
    features,
    filter_one,
    filter_two,
    readout_in,
    readout_out,
    charge_weight,
    neighbour_blocks,
    live_slots,
    wave_ints,
):
    local_atoms = positions.shape[1]
    block_count = neighbour_blocks.shape[0]
    block_size = local_atoms // block_count
    slot_count = neighbour_blocks.shape[1]
    atom_rank = lax.axis_index("atoms")
    device_count = lax.axis_size("atoms")
    near_ids = neighbour_blocks - (atom_rank - 1) * block_count
    live_mask = jnp.arange(slot_count)[None, :] < live_slots[:, None]
    widened_first = widen_rows(jnp.concatenate([positions, features], axis=0))
    wide_pos = widened_first[:3]
    wide_features = widened_first[3:]

    def first_layer(centre_pos, near_pos):
        return features + messages(
            centre_pos, near_pos, wide_features, filter_one, near_ids, live_mask, block_size
        )

    z_one_part, back_first = jax.vjp(first_layer, positions, wide_pos)
    wide_z = widen_rows(z_one_part)

    def second_layer(centre_pos, near_pos, near_values, values):
        return values + messages(
            centre_pos, near_pos, near_values, filter_two, near_ids, live_mask, block_size
        )

    z_two_part, back_second = jax.vjp(second_layer, positions, wide_pos, wide_z, z_one_part)

    def readout_energy(values):
        hidden = jnp.dot(readout_in.T, values, precision=highest)
        return jnp.sum(jax.nn.silu(hidden) * readout_out[:, None])

    short_grad = jax.grad(readout_energy)(z_two_part)
    charges = jnp.dot(charge_weight.T, z_two_part, precision=highest)
    depth_side = local_atoms / (atom_density * slab_width * slab_height)
    scales = jnp.array(
        [
            2.0 * math.pi / (slab_width * device_count),
            2.0 * math.pi / slab_height,
            2.0 * math.pi / depth_side,
        ],
        jnp.float32,
    )
    waves = wave_ints.astype(jnp.float32) * scales[:, None]
    squared = jnp.sum(waves * waves, axis=0)
    wave_weight = jnp.exp(-0.5 * spread_square * squared) / (squared + screen_square)
    phases = jnp.dot(waves.T, positions, precision=highest)
    cosine_table = jnp.cos(phases)
    sine_table = jnp.sin(phases)
    cosine_part = jnp.dot(charges, cosine_table.T, precision=highest)
    sine_part = jnp.dot(charges, sine_table.T, precision=highest)
    cosine_sum, sine_sum = lax.psum((cosine_part, sine_part), "atoms")
    factor = 2.0 / (local_atoms * device_count)
    cosine_scaled = cosine_sum * wave_weight[None, :] * factor
    sine_scaled = sine_sum * wave_weight[None, :] * factor
    charge_grad = jnp.dot(cosine_scaled, cosine_table, precision=highest) + jnp.dot(
        sine_scaled, sine_table, precision=highest
    )
    phase_grad = cosine_table * jnp.dot(
        sine_scaled.T, charges, precision=highest
    ) - sine_table * jnp.dot(cosine_scaled.T, charges, precision=highest)
    wave_force = jnp.dot(waves, phase_grad, precision=highest)
    charge_grad, wave_force = lax.psum((charge_grad, wave_force), "kvec")
    z_two_grad = jnp.dot(charge_weight, charge_grad, precision=highest) + short_grad
    own_second, wide_second, wide_z_grad, z_one_grad_part = back_second(z_two_grad)
    returned_second = send_back(jnp.concatenate([wide_second, wide_z_grad], axis=0))
    z_one_grad = z_one_grad_part + returned_second[3:]
    own_first, wide_first_grad = back_first(z_one_grad)
    returned_first = send_back(wide_first_grad)
    short_force = own_second + returned_second[:3] + own_first + returned_first
    return -(short_force + wave_force)


def solution(mesh):
    in_specs = (
        P(None, "atoms"),
        P(None, "atoms"),
        P(),
        P(),
        P(),
        P(),
        P(),
        P("atoms", None),
        P("atoms"),
        P(None, "kvec"),
    )
    out_specs = P(None, "atoms")
    return jax.shard_map(body, mesh=mesh, in_specs=in_specs, out_specs=out_specs, check_vma=False)
```

profile of v0, /device:TPU:0, one launch (start us, length us, event | category | flops | bytes accessed | tf_op | source)
XLA Modules:
  0.0 627.5 jit_solution(11410766735486424098)
XLA Ops:
  11.6 21.7 %fusion.175 = (f32[2048,512]{1,0:T(8,128)}, f32[2048,512]{1,0:T(8,128)}) fusion(f32[3,512]{1,0:T(4,128)} %param.23, s32[3,2048]{1,0:T(4,128)} %param.32, f32[3]{0:T(128)} %constant.632.clone), kind=kOutput, calls=%fused_computation.299 | convolution fusion | flops 37761024 | bytes 8419340 | tf_op jit(solution)/shard_map/dot_general | solution.py:152
  34.2 75.1 %while.66 = (s32[]{:T(128)}, f32[4,64,128]{2,1,0:T(8,128)}, s32[4]{0:T(128)S(1)}, s32[4,9]{1,0:T(4,128)S(1)}, f32[64,12,128]{2,0,1:T(8,128)S(1)}, /*index=5*/f32...) while((s32[]{:T(128)}, f32[4,64,128]{2,1,0:T(8,128)}, ...), condition=%wide.region_2.4_spmd.clone, body=%wide.region_0.3_spmd.clone.sunk | while | flops 1827894784 | bytes 6889634 | solution.py:78
  40.9 10.7 %fusion.252 = f32[16,64,128]{2,1,0:T(8,128)S(1)} fusion(f32[128,9,128]{2,0,1:T(8,128)S(1)} %fusion.250, f32[16]{0:T(128)S(1)} %multiply_bitcast_fusion.9, f32[128,9,128]{2,0,1:T(8,128)S(1)} %get-tuple-element.1581, f32[128,9,128]{2,0,1:T(8,128)S(1)} %get-tuple-element.1582, f32[9,64,128]{2,1,0:T(8,128)S(1)} %gather_fusion.1, ...), kind=kOutput, calls=%fused_computation.30.clone.1 | convolution fusion | flops 1823809536 | bytes 2588745 | tf_op jit(solution)/shard_map/jvp()/while/body/eval_jaxpr/mij,fj->mfi/dot_general | solution.py:61
  59.6 10.7 %fusion.252 = f32[16,64,128]{2,1,0:T(8,128)S(1)} fusion(f32[128,9,128]{2,0,1:T(8,128)S(1)} %fusion.250, f32[16]{0:T(128)S(1)} %multiply_bitcast_fusion.9, f32[128,9,128]{2,0,1:T(8,128)S(1)} %get-tuple-element.1581, f32[128,9,128]{2,0,1:T(8,128)S(1)} %get-tuple-element.1582, f32[9,64,128]{2,1,0:T(8,128)S(1)} %gather_fusion.1, ...), kind=kOutput, calls=%fused_computation.30.clone.1 | convolution fusion | flops 1823809536 | bytes 2588745 | tf_op jit(solution)/shard_map/jvp()/while/body/eval_jaxpr/mij,fj->mfi/dot_general | solution.py:61
  78.3 10.7 %fusion.252 = f32[16,64,128]{2,1,0:T(8,128)S(1)} fusion(f32[128,9,128]{2,0,1:T(8,128)S(1)} %fusion.250, f32[16]{0:T(128)S(1)} %multiply_bitcast_fusion.9, f32[128,9,128]{2,0,1:T(8,128)S(1)} %get-tuple-element.1581, f32[128,9,128]{2,0,1:T(8,128)S(1)} %get-tuple-element.1582, f32[9,64,128]{2,1,0:T(8,128)S(1)} %gather_fusion.1, ...), kind=kOutput, calls=%fused_computation.30.clone.1 | convolution fusion | flops 1823809536 | bytes 2588745 | tf_op jit(solution)/shard_map/jvp()/while/body/eval_jaxpr/mij,fj->mfi/dot_general | solution.py:61
  97.0 10.7 %fusion.252 = f32[16,64,128]{2,1,0:T(8,128)S(1)} fusion(f32[128,9,128]{2,0,1:T(8,128)S(1)} %fusion.250, f32[16]{0:T(128)S(1)} %multiply_bitcast_fusion.9, f32[128,9,128]{2,0,1:T(8,128)S(1)} %get-tuple-element.1581, f32[128,9,128]{2,0,1:T(8,128)S(1)} %get-tuple-element.1582, f32[9,64,128]{2,1,0:T(8,128)S(1)} %gather_fusion.1, ...), kind=kOutput, calls=%fused_computation.30.clone.1 | convolution fusion | flops 1823809536 | bytes 2588745 | tf_op jit(solution)/shard_map/jvp()/while/body/eval_jaxpr/mij,fj->mfi/dot_general | solution.py:61
  110.3 4.8 collective-permute-start.2
  119.8 73.4 %while.67 = (s32[]{:T(128)}, f32[4,64,128]{2,1,0:T(8,128)S(1)}, s32[4]{0:T(128)S(1)}, s32[4,9]{1,0:T(4,128)S(1)}, f32[64,12,128]{2,0,1:T(8,128)S(1)}, /*index=5*...) while((s32[]{:T(128)}, f32[4,64,128]{2,1,0:T(8,128)S(1)}, ...), condition=%wide.region_5.7_spmd.clone, body=%wide.region_3.6_spmd.clone.sunk | while | flops 1827894784 | bytes 6889126 | solution.py:78
  126.8 10.7 %fusion.260 = f32[16,64,128]{2,1,0:T(8,128)S(1)} fusion(f32[128,9,128]{2,0,1:T(8,128)S(1)} %fusion.258, f32[16]{0:T(128)S(1)} %multiply_bitcast_fusion.10, f32[128,9,128]{2,0,1:T(8,128)S(1)} %get-tuple-element.1596, f32[128,9,128]{2,0,1:T(8,128)S(1)} %get-tuple-element.1597, f32[9,64,128]{2,1,0:T(8,128)S(1)} %gather_fusion.3, ...), kind=kOutput, calls=%fused_computation.68.clone.1 | convolution fusion | flops 1823809536 | bytes 2588745 | tf_op jit(solution)/shard_map/jvp()/while/body/eval_jaxpr/mij,fj->mfi/dot_general | solution.py:61
  144.9 10.7 %fusion.260 = f32[16,64,128]{2,1,0:T(8,128)S(1)} fusion(f32[128,9,128]{2,0,1:T(8,128)S(1)} %fusion.258, f32[16]{0:T(128)S(1)} %multiply_bitcast_fusion.10, f32[128,9,128]{2,0,1:T(8,128)S(1)} %get-tuple-element.1596, f32[128,9,128]{2,0,1:T(8,128)S(1)} %get-tuple-element.1597, f32[9,64,128]{2,1,0:T(8,128)S(1)} %gather_fusion.3, ...), kind=kOutput, calls=%fused_computation.68.clone.1 | convolution fusion | flops 1823809536 | bytes 2588745 | tf_op jit(solution)/shard_map/jvp()/while/body/eval_jaxpr/mij,fj->mfi/dot_general | solution.py:61
  163.1 10.7 %fusion.260 = f32[16,64,128]{2,1,0:T(8,128)S(1)} fusion(f32[128,9,128]{2,0,1:T(8,128)S(1)} %fusion.258, f32[16]{0:T(128)S(1)} %multiply_bitcast_fusion.10, f32[128,9,128]{2,0,1:T(8,128)S(1)} %get-tuple-element.1596, f32[128,9,128]{2,0,1:T(8,128)S(1)} %get-tuple-element.1597, f32[9,64,128]{2,1,0:T(8,128)S(1)} %gather_fusion.3, ...), kind=kOutput, calls=%fused_computation.68.clone.1 | convolution fusion | flops 1823809536 | bytes 2588745 | tf_op jit(solution)/shard_map/jvp()/while/body/eval_jaxpr/mij,fj->mfi/dot_general | solution.py:61
  181.3 10.7 %fusion.260 = f32[16,64,128]{2,1,0:T(8,128)S(1)} fusion(f32[128,9,128]{2,0,1:T(8,128)S(1)} %fusion.258, f32[16]{0:T(128)S(1)} %multiply_bitcast_fusion.10, f32[128,9,128]{2,0,1:T(8,128)S(1)} %get-tuple-element.1596, f32[128,9,128]{2,0,1:T(8,128)S(1)} %get-tuple-element.1597, f32[9,64,128]{2,1,0:T(8,128)S(1)} %gather_fusion.3, ...), kind=kOutput, calls=%fused_computation.68.clone.1 | convolution fusion | flops 1823809536 | bytes 2588745 | tf_op jit(solution)/shard_map/jvp()/while/body/eval_jaxpr/mij,fj->mfi/dot_general | solution.py:61
  194.5 6.4 %fusion.178 = f32[16,2048]{1,0:T(8,128)} fusion(f32[512,16]{0,1:T(8,128)S(1)} %fusion.161, f32[2048,512]{1,0:T(8,128)} %get-tuple-element.1291), kind=kOutput, calls=%fused_computation.302 | convolution fusion | flops 201326592 | bytes 4358144 | tf_op jit(solution)/shard_map/dot_general | solution.py:156
  200.8 4.2 fusion.177
  205.4 110.3 %all-reduce.4.cloned.1.call-done = (f32[16,2048]{1,0:T(8,128)}, f32[16,2048]{1,0:T(8,128)}) async-done(((f32[16,2048]{1,0:T(8,128)}, f32[16,2048]{1,0:T(8,128)}), (f32[16,2048]{1,0:T(8,128)}, f32[16,2048]{1,0:T(8,128)})) %all-reduce.4.cloned.1.call-update) | async-done | bytes 262160 | tf_op jit(solution)/shard_map/psum | solution.py:157
  315.8 4.4 fusion.146
  332.3 18.1 %all-reduce.1 = (f32[3,512]{1,0:T(4,128)}, f32[16,512]{1,0:T(8,128)S(1)}) all-reduce(f32[3,512]{1,0:T(4,128)S(1)} %fusion.126, f32[16,512]{1,0:T(8,128)S(1)} %convolution_add_fusion.1), channel_id=1, replica_groups=mesh['atoms'=32,'kvec'=4] {'kvec'}, use_global_device_ids=true, to_apply=%region_27.30 | all-reduce | flops 9728 | bytes 77824 | tf_op jit(solution)/shard_map/psum | solution.py:168
  351.9 164.1 %while.68 = (s32[]{:T(128)}, f32[3,4,128]{2,0,1:T(4,128)S(1)}, f32[3,12,128]{2,0,1:T(4,128)S(1)}, f32[64,12,128]{2,0,1:T(8,128)S(1)}, s32[4]{0:T(128)S(1)}, /*in...) while((s32[]{:T(128)}, f32[3,4,128]{2,0,1:T(4,128)S(1)}, ...), condition=%wide.region_18.21_spmd.clone, body=%wide.region_10.20_spmd.clone.sunk | while | flops 3671647232 | bytes 17249436 | solution.py:78
  362.4 10.5 %fusion.272 = f32[9,64,128]{2,1,0:T(8,128)S(1)} fusion(f32[9,128,128]{2,1,0:T(8,128)S(1)} %bitcast.449, f32[16]{0:T(128)S(1)} %convert_multiply_fusion.7, f32[9,128,128]{2,1,0:T(8,128)S(1)} %bitcast.447, f32[9,128,128]{2,1,0:T(8,128)S(1)} %bitcast.448, f32[64,128]{1,0:T(8,128)S(1)} %dynamic-slice_bitcast_fusion.24, f32[64,16]{0,1:T(8,128)S(1)} %bitcast.458), kind=kOutput, calls=%fused_computation.121.clone.1 | convolution fusion | flops 1823866880 | bytes 2101312 | tf_op jit(solution)/shard_map/transpose(jvp())/while/body/eval_jaxpr/checkpoint/mij,fj->mfi/dot_general | solution.py:61
  375.8 13.4 %fusion.267 = (f32[128,9,128]{2,0,1:T(8,128)S(1)}, f32[128,9,128]{2,0,1:T(8,128)S(1)}) fusion(f32[16]{0:T(128)S(1)} %convert_multiply_fusion.7, f32[128,9,128]{2,0,1:T(8,128)S(1)} %get-tuple-element.1616, f32[128,9,128]{2,0,1:T(8,128)} %copy.159, f32[128,9,128]{2,0,1:T(8,128)} %get-tuple-element.1619, ...), kind=kOutput, calls=%fused_computation.102.clone.1 | convolution fusion | flops 1840160768 | bytes 3282112 | tf_op jit(solution)/shard_map/transpose(jvp())/while/body/eval_jaxpr/checkpoint/mij,fj->mfi/dot_general | solution.py:61
  403.3 10.5 %fusion.272 = f32[9,64,128]{2,1,0:T(8,128)S(1)} fusion(f32[9,128,128]{2,1,0:T(8,128)S(1)} %bitcast.449, f32[16]{0:T(128)S(1)} %convert_multiply_fusion.7, f32[9,128,128]{2,1,0:T(8,128)S(1)} %bitcast.447, f32[9,128,128]{2,1,0:T(8,128)S(1)} %bitcast.448, f32[64,128]{1,0:T(8,128)S(1)} %dynamic-slice_bitcast_fusion.24, f32[64,16]{0,1:T(8,128)S(1)} %bitcast.458), kind=kOutput, calls=%fused_computation.121.clone.1 | convolution fusion | flops 1823866880 | bytes 2101312 | tf_op jit(solution)/shard_map/transpose(jvp())/while/body/eval_jaxpr/checkpoint/mij,fj->mfi/dot_general | solution.py:61
  416.8 13.4 %fusion.267 = (f32[128,9,128]{2,0,1:T(8,128)S(1)}, f32[128,9,128]{2,0,1:T(8,128)S(1)}) fusion(f32[16]{0:T(128)S(1)} %convert_multiply_fusion.7, f32[128,9,128]{2,0,1:T(8,128)S(1)} %get-tuple-element.1616, f32[128,9,128]{2,0,1:T(8,128)} %copy.159, f32[128,9,128]{2,0,1:T(8,128)} %get-tuple-element.1619, ...), kind=kOutput, calls=%fused_computation.102.clone.1 | convolution fusion | flops 1840160768 | bytes 3282112 | tf_op jit(solution)/shard_map/transpose(jvp())/while/body/eval_jaxpr/checkpoint/mij,fj->mfi/dot_general | solution.py:61
  444.2 10.5 %fusion.272 = f32[9,64,128]{2,1,0:T(8,128)S(1)} fusion(f32[9,128,128]{2,1,0:T(8,128)S(1)} %bitcast.449, f32[16]{0:T(128)S(1)} %convert_multiply_fusion.7, f32[9,128,128]{2,1,0:T(8,128)S(1)} %bitcast.447, f32[9,128,128]{2,1,0:T(8,128)S(1)} %bitcast.448, f32[64,128]{1,0:T(8,128)S(1)} %dynamic-slice_bitcast_fusion.24, f32[64,16]{0,1:T(8,128)S(1)} %bitcast.458), kind=kOutput, calls=%fused_computation.121.clone.1 | convolution fusion | flops 1823866880 | bytes 2101312 | tf_op jit(solution)/shard_map/transpose(jvp())/while/body/eval_jaxpr/checkpoint/mij,fj->mfi/dot_general | solution.py:61
  457.7 13.4 %fusion.267 = (f32[128,9,128]{2,0,1:T(8,128)S(1)}, f32[128,9,128]{2,0,1:T(8,128)S(1)}) fusion(f32[16]{0:T(128)S(1)} %convert_multiply_fusion.7, f32[128,9,128]{2,0,1:T(8,128)S(1)} %get-tuple-element.1616, f32[128,9,128]{2,0,1:T(8,128)} %copy.159, f32[128,9,128]{2,0,1:T(8,128)} %get-tuple-element.1619, ...), kind=kOutput, calls=%fused_computation.102.clone.1 | convolution fusion | flops 1840160768 | bytes 3282112 | tf_op jit(solution)/shard_map/transpose(jvp())/while/body/eval_jaxpr/checkpoint/mij,fj->mfi/dot_general | solution.py:61
  485.2 10.5 %fusion.272 = f32[9,64,128]{2,1,0:T(8,128)S(1)} fusion(f32[9,128,128]{2,1,0:T(8,128)S(1)} %bitcast.449, f32[16]{0:T(128)S(1)} %convert_multiply_fusion.7, f32[9,128,128]{2,1,0:T(8,128)S(1)} %bitcast.447, f32[9,128,128]{2,1,0:T(8,128)S(1)} %bitcast.448, f32[64,128]{1,0:T(8,128)S(1)} %dynamic-slice_bitcast_fusion.24, f32[64,16]{0,1:T(8,128)S(1)} %bitcast.458), kind=kOutput, calls=%fused_computation.121.clone.1 | convolution fusion | flops 1823866880 | bytes 2101312 | tf_op jit(solution)/shard_map/transpose(jvp())/while/body/eval_jaxpr/checkpoint/mij,fj->mfi/dot_general | solution.py:61
  498.6 13.4 %fusion.267 = (f32[128,9,128]{2,0,1:T(8,128)S(1)}, f32[128,9,128]{2,0,1:T(8,128)S(1)}) fusion(f32[16]{0:T(128)S(1)} %convert_multiply_fusion.7, f32[128,9,128]{2,0,1:T(8,128)S(1)} %get-tuple-element.1616, f32[128,9,128]{2,0,1:T(8,128)} %copy.159, f32[128,9,128]{2,0,1:T(8,128)} %get-tuple-element.1619, ...), kind=kOutput, calls=%fused_computation.102.clone.1 | convolution fusion | flops 1840160768 | bytes 3282112 | tf_op jit(solution)/shard_map/transpose(jvp())/while/body/eval_jaxpr/checkpoint/mij,fj->mfi/dot_general | solution.py:61
  522.5 90.4 %while.69 = (s32[]{:T(128)}, f32[3,4,128]{2,0,1:T(4,128)S(1)}, f32[3,12,128]{2,0,1:T(4,128)S(1)}, s32[4]{0:T(128)S(1)}, f32[4,64,128]{2,1,0:T(8,128)S(1)}, /*ind...) while((s32[]{:T(128)}, f32[3,4,128]{2,0,1:T(4,128)S(1)}, ...), condition=%wide.region_26.29_spmd.clone, body=%wide.region_19.28_spmd.clone.sunk | while | flops 1846526848 | bytes 10113567 | solution.py:78
  529.2 12.2 %fusion.277 = (f32[128,9,128]{2,0,1:T(8,128)S(1)}, f32[128,9,128]{2,0,1:T(8,128)S(1)}) fusion(f32[16]{0:T(128)S(1)} %convert_multiply_fusion.8, f32[128,9,128]{2,0,1:T(8,128)S(1)} %get-tuple-element.1644, f32[128,9,128]{2,0,1:T(8,128)S(1)} %and_convert_fusion.5, f32[128,9,128]{2,0,1:T(8,128)S(1)} %get-tuple-element.1647, ...), kind=kOutput, calls=%fused_computation.178.clone.1 | convolution fusion | flops 1840160768 | bytes 3282112 | tf_op jit(solution)/shard_map/transpose(jvp())/while/body/eval_jaxpr/checkpoint/mij,fj->mfi/dot_general | solution.py:61
  551.8 12.2 %fusion.277 = (f32[128,9,128]{2,0,1:T(8,128)S(1)}, f32[128,9,128]{2,0,1:T(8,128)S(1)}) fusion(f32[16]{0:T(128)S(1)} %convert_multiply_fusion.8, f32[128,9,128]{2,0,1:T(8,128)S(1)} %get-tuple-element.1644, f32[128,9,128]{2,0,1:T(8,128)S(1)} %and_convert_fusion.5, f32[128,9,128]{2,0,1:T(8,128)S(1)} %get-tuple-element.1647, ...), kind=kOutput, calls=%fused_computation.178.clone.1 | convolution fusion | flops 1840160768 | bytes 3282112 | tf_op jit(solution)/shard_map/transpose(jvp())/while/body/eval_jaxpr/checkpoint/mij,fj->mfi/dot_general | solution.py:61
  574.4 12.2 %fusion.277 = (f32[128,9,128]{2,0,1:T(8,128)S(1)}, f32[128,9,128]{2,0,1:T(8,128)S(1)}) fusion(f32[16]{0:T(128)S(1)} %convert_multiply_fusion.8, f32[128,9,128]{2,0,1:T(8,128)S(1)} %get-tuple-element.1644, f32[128,9,128]{2,0,1:T(8,128)S(1)} %and_convert_fusion.5, f32[128,9,128]{2,0,1:T(8,128)S(1)} %get-tuple-element.1647, ...), kind=kOutput, calls=%fused_computation.178.clone.1 | convolution fusion | flops 1840160768 | bytes 3282112 | tf_op jit(solution)/shard_map/transpose(jvp())/while/body/eval_jaxpr/checkpoint/mij,fj->mfi/dot_general | solution.py:61
  597.0 12.2 %fusion.277 = (f32[128,9,128]{2,0,1:T(8,128)S(1)}, f32[128,9,128]{2,0,1:T(8,128)S(1)}) fusion(f32[16]{0:T(128)S(1)} %convert_multiply_fusion.8, f32[128,9,128]{2,0,1:T(8,128)S(1)} %get-tuple-element.1644, f32[128,9,128]{2,0,1:T(8,128)S(1)} %and_convert_fusion.5, f32[128,9,128]{2,0,1:T(8,128)S(1)} %get-tuple-element.1647, ...), kind=kOutput, calls=%fused_computation.178.clone.1 | convolution fusion | flops 1840160768 | bytes 3282112 | tf_op jit(solution)/shard_map/transpose(jvp())/while/body/eval_jaxpr/checkpoint/mij,fj->mfi/dot_general | solution.py:61
  614.2 4.0 collective-permute-start.7
  (472 shorter events, 174.4 us)
Async XLA Ops:
  6.5 198.6 %copy-start = (f32[64,64]{1,0:T(8,128)S(1)}, f32[64,64]{1,0:T(8,128)}, u32[]{:S(2)}) copy-start(f32[64,64]{1,0:T(8,128)} %param.27) | copy-start | bytes 49156
  6.5 309.2 %all-reduce.4.cloned.1.call-start = ((), (), s32[]{:S(2)}) async-start(), calls=%async_computation | async-start | bytes 524288 | tf_op jit(solution)/shard_map/psum | solution.py:157
  7.5 25.9 %collective-permute-start = (f32[67,512]{1,0:T(8,128)S(1)}, f32[67,512]{1,0:T(8,128)S(1)}, u32[]{:S(2)}, u32[]{:S(2)}) collective-permute-start(f32[67,512]{1,0:T(8,128)S(1)} %pad_maximum_fusion.2), channel_id=1, source_target_pairs={{0,4},{4,8},{8,12},{12,16},{16,20},{20,24},{24,28},{28,32},{32,36}... | collective-permute-start | bytes 411656 | tf_op jit(solution)/shard_map/ppermute | solution.py:25
  8.8 24.6 %collective-permute-start.1 = (f32[67,512]{1,0:T(8,128)S(1)}, f32[67,512]{1,0:T(8,128)S(1)}, u32[]{:S(2)}, u32[]{:S(2)}) collective-permute-start(f32[67,512]{1,0:T(8,128)S(1)} %pad_maximum_fusion.2), channel_id=1, source_target_pairs={{4,0},{8,4},{12,8},{16,12},{20,16},{24,20},{28,24},{32,28},{36,32}... | collective-permute-start | bytes 411656 | tf_op jit(solution)/shard_map/ppermute | solution.py:26
  11.5 21.8 %copy-start.14 = (s32[3,2048]{1,0:T(4,128)S(1)}, s32[3,2048]{1,0:T(4,128)}, u32[]{:S(2)}) copy-start(s32[3,2048]{1,0:T(4,128)} %param.32) | copy-start | bytes 73732
  11.5 21.8 %copy-start.20 = (f32[3]{0:T(128)S(1)}, f32[3]{0:T(128)}, u32[]{:S(2)}) copy-start(f32[3]{0:T(128)} %constant.632.clone) | copy-start | bytes 40
  11.5 21.9 %copy-start.6 = (f32[64,512]{1,0:T(8,128)S(1)}, f32[64,512]{1,0:T(8,128)}, u32[]{:S(2)}) copy-start(f32[64,512]{1,0:T(8,128)} %param.24) | copy-start | bytes 393220
  11.5 21.9 %copy-start.9 = (f32[3,512]{1,0:T(4,128)S(1)}, f32[3,512]{1,0:T(4,128)}, u32[]{:S(2)}) copy-start(f32[3,512]{1,0:T(4,128)} %param.23) | copy-start | bytes 18436
  11.5 22.7 %copy-start.16 = (f32[16,64]{1,0:T(8,128)S(1)}, f32[16,64]{1,0:T(8,128)}, u32[]{:S(2)}) copy-start(f32[16,64]{1,0:T(8,128)} %param.25) | copy-start | bytes 12292
  34.2 85.5 %copy-start.15 = (f32[16,64]{1,0:T(8,128)S(1)}, f32[16,64]{1,0:T(8,128)}, u32[]{:S(2)}) copy-start(f32[16,64]{1,0:T(8,128)} %param.26) | copy-start | bytes 12292
  109.3 10.5 %copy-start.1 = (f32[64,12,128]{2,0,1:T(8,128)}, f32[64,12,128]{2,0,1:T(8,128)S(1)}, u32[]{:S(2)}) copy-start(f32[64,12,128]{2,0,1:T(8,128)S(1)} %get-tuple-element.1836) | copy-start | bytes 1179652
  110.3 9.4 %copy-start.7 = (f32[64,512]{1,0:T(8,128)}, f32[64,512]{1,0:T(8,128)S(1)}, u32[]{:S(2)}) copy-start(f32[64,512]{1,0:T(8,128)S(1)} %bitcast_add_fusion.3) | copy-start | bytes 393220
  110.3 6.2 collective-permute-start.2
  115.2 4.5 collective-permute-start.3
  119.8 73.4 %copy-start.18 = (f32[64,16]{0,1:T(8,128)S(1)}, f32[64,16]{0,1:T(8,128)}, u32[]{:S(2)}) copy-start(f32[64,16]{0,1:T(8,128)} %param.29) | copy-start | bytes 12292
  193.2 7.7 %copy-start.3 = (f32[2048,512]{1,0:T(8,128)S(1)}, f32[2048,512]{1,0:T(8,128)}, u32[]{:S(2)}) copy-start(f32[2048,512]{1,0:T(8,128)} %get-tuple-element.1290) | copy-start | bytes 12582916
  194.5 10.6 %copy-start.8 = (f32[64,512]{1,0:T(8,128)S(1)}, f32[64,512]{1,0:T(8,128)}, u32[]{:S(2)}) copy-start(f32[64,512]{1,0:T(8,128)} %copy-done.7) | copy-start | bytes 393220
  315.8 4.4 copy-start.12
  315.8 7.9 %copy-start.11 = (f32[16,2048]{1,0:T(8,128)S(1)}, f32[16,2048]{1,0:T(8,128)}, u32[]{:S(2)}) copy-start(f32[16,2048]{1,0:T(8,128)} %get-tuple-element.1269) | copy-start | bytes 393220
  320.2 7.4 %copy-start.5 = (f32[2048,512]{1,0:T(8,128)S(1)}, f32[2048,512]{1,0:T(8,128)}, u32[]{:S(2)}) copy-start(f32[2048,512]{1,0:T(8,128)} %get-tuple-element.1291) | copy-start | bytes 12582916
  323.7 6.1 copy-start.4
  329.7 21.0 %copy-start.21 = (f32[64]{0:T(128)S(1)}, f32[64]{0:T(128)}, u32[]{:S(2)}) copy-start(f32[64]{0:T(128)} %param.28) | copy-start | bytes 772
  329.7 22.1 %copy-start.22 = (s32[4]{0:T(128)S(1)}, s32[4]{0:T(128)}, u32[]{:S(2)}) copy-start(s32[4]{0:T(128)} %param.31) | copy-start | bytes 52
  351.1 0.7 copy-start.13
  351.9 170.6 %copy-start.2 = (f32[64,12,128]{2,0,1:T(8,128)S(1)}, f32[64,12,128]{2,0,1:T(8,128)}, u32[]{:S(2)}) copy-start(f32[64,12,128]{2,0,1:T(8,128)} %copy-done.1) | copy-start | bytes 1179652
  351.9 170.6 %copy-start.17 = (f32[16,64]{1,0:T(8,128)S(1)}, f32[16,64]{1,0:T(8,128)}, u32[]{:S(2)}) copy-start(f32[16,64]{1,0:T(8,128)} %param.25) | copy-start | bytes 12292
  516.1 4.3 collective-permute-start.4
  517.4 4.0 collective-permute-start.5
  521.4 1.1 copy-start.10
  522.5 96.6 %copy-start.19 = (f32[3,512]{1,0:T(4,128)S(1)}, f32[3,512]{1,0:T(4,128)}, u32[]{:S(2)}) copy-start(f32[3,512]{1,0:T(4,128)} %get-tuple-element.1270) | copy-start | bytes 18436
  612.9 5.4 collective-permute-start.6
  614.2 4.9 collective-permute-start.7
Sparse Core Ops, SparseCore 0:
  205.2 110.4 all-reduce.3
where the time goes:
time: 639 us; the launch traced here: 628 us
  matrix products  288 us (45%)
  waiting for transfers between devices  115 us (18%)
  other arithmetic  95.8 us (15%)
  local copies, waits for them, and re-layouts  42.7 us (7%)
  loops' own time  34.9 us (5%)
  starting transfers between devices  18.4 us (3%)
  blocking collectives  18.1 us (3%)
  between operations  14.2 us (2%)
    dot_general x20, matrix products, block_messages(): jnp.einsum('mij,fj->mfi', radial_terms, values, precision=highest)  230 us
    psum x1, waiting for transfers between devices, body(): cosine_sum, sine_sum = lax.psum((cosine_part, sine_part), 'atoms')  110 us
    select_n x20, other arithmetic, radial(): jnp.where(distance < cutoff_radius, 0.5 * (jnp.cos(jnp.pi * distance / cu...  45.8 us
    another operation x4, loops' own time, messages(): lax.map(jax.checkpoint(per_block), jnp.arange(block_count, dtype=jnp.int32))  34.9 us
    dot_general x1, matrix products, body(): phases = jnp.dot(waves.T, positions, precision=highest)  21.7 us
    mul x8, other arithmetic, block_messages(): distance = jnp.sqrt(jnp.sum(offset * offset, axis=0) + self_offset)  18.3 us
    psum x1, blocking collectives, body(): charge_grad, wave_force = lax.psum((charge_grad, wave_force), 'kvec')  18.1 us
  transfers between devices with their start and end apart: 9, of which 4 were waited for; matrix products, arithmetic and copies ran while one was open for 4% of the time, Pallas kernels for 0%

commit v1 on v0

v1 whole, which is shorter than its diff:
```python
import functools
import math

import jax
import jax.numpy as jnp
import numpy as np
from jax import lax
from jax.experimental import pallas as pl
from jax.experimental.pallas import tpu as pltpu
from jax.sharding import PartitionSpec as P

MESH = pl.DeviceIdType.MESH
highest = lax.Precision.HIGHEST
f32 = jnp.float32
bf16 = jnp.bfloat16
slab_width = 5.0
slab_height = 10.0
atom_density = 0.1
cutoff_radius = 5.0
self_offset = 0.0001
screen_square = 0.25
spread_square = 1.0


def trig_coefficients():
    u = 0.5 * np.cos(np.pi * (np.arange(4000) + 0.5) / 8000)
    cheb = np.polynomial.chebyshev
    scaled = 8.0 * u * u - 1.0
    out = []
    for values, degree, weight in (
        (np.sin(2 * np.pi * u) / u, 6, u),
        (np.cos(2 * np.pi * u), 6, np.ones_like(u)),
    ):
        fitted = cheb.Chebyshev(cheb.chebfit(scaled, values, degree, w=weight))
        poly = fitted.convert(kind=np.polynomial.Polynomial)
        shifted = poly(np.polynomial.Polynomial([-1.0, 8.0]))
        out.append([float(c) for c in shifted.coef])
    return out


SIN_COEF, COS_COEF = trig_coefficients()


def sin_cos_turns(u):
    square = u * u
    sine = SIN_COEF[-1]
    for c in SIN_COEF[-2::-1]:
        sine = sine * square + c
    cosine = COS_COEF[-1]
    for c in COS_COEF[-2::-1]:
        cosine = cosine * square + c
    return sine * u, cosine


def split(x):
    high = x.astype(bf16)
    return high, (x - high.astype(f32)).astype(bf16)


def dot_nt(a, b):
    return lax.dot_general(a, b, (((1,), (1,)), ((), ())), preferred_element_type=f32)


def dot_nn(a, b):
    return lax.dot_general(a, b, (((1,), (0,)), ((), ())), preferred_element_type=f32)


def exact_nn(a, b):
    return lax.dot_general(
        a, b, (((1,), (0,)), ((), ())), precision=highest, preferred_element_type=f32
    )


def exact_tn(a, b):
    return lax.dot_general(
        a, b, (((0,), (0,)), ((), ())), precision=highest, preferred_element_type=f32
    )


def kernel(
    sizes,
    pos_ref, feat_ref, f1_ref, f2_ref, rin_ref, rout_ref, cw_ref, wave_ref, nb_ref, live_ref,
    out_ref,
    wide, zwide, post, xpad, own_t, nf, wtab, thi, tlo, ahi, alo, zf, zz, geo,
    wd1, wd2, wcol, gwt, gw, bbuf, qsum, tslot, tsend, trecv, qbuf, sfb, rsb, agb, rmat,
    cgs, cgr, wf, pg, fsend, frecv, inv,
    ssem, rsem, halo_r,
):
    n_at, n_k, n_blk, bs, n_slot, n_f, n_m, n_q, n_wave = sizes
    total_atoms = n_at * n_blk * bs
    p = lax.axis_index("atoms")
    q = lax.axis_index("kvec")
    half_m = n_m // 2
    wide_n = n_slot * bs
    k_chunks = n_wave // bs
    near_peers = [(dp, dq) for dp in (-1, 0, 1) for dq in range(n_k) if (dp, dq) != (0, 0)]

    def peer(dp, dq):
        return {"atoms": lax.rem(p + dp + n_at, n_at), "kvec": lax.rem(q + dq, n_k)}

    def send(src, dst, which, dp, dq, recv=None):
        copy = pltpu.make_async_remote_copy(
            src_ref=src, dst_ref=dst, send_sem=ssem.at[which],
            recv_sem=rsem.at[which] if recv is None else recv,
            device_id=peer(dp, dq), device_id_type=MESH,
        )
        copy.start()

    def wait_bytes(ref, sem):
        pltpu.make_async_copy(ref, ref, sem).wait()

    barrier = pltpu.get_barrier_semaphore()
    partners = near_peers + [(d, 0) for d in range(2, n_at - 1)]
    for dp, dq in partners:
        pl.semaphore_signal(barrier, inc=1, device_id=peer(dp, dq), device_id_type=MESH)

    for c in range(n_blk):
        lanes = slice(c * bs, (c + 1) * bs)
        wide[n_blk + c, 0:n_f, :] = feat_ref[:, lanes]
        wide[n_blk + c, n_f:, :] = jnp.zeros((8, bs), f32)
        wide[n_blk + c, n_f : n_f + 3, :] = pos_ref[:, lanes]
    pl.semaphore_wait(barrier, len(partners))
    own_rows = wide.at[pl.ds(n_blk, n_blk)]
    send(own_rows, wide.at[pl.ds(0, n_blk)], 0, 1, 0, halo_r.at[0])
    send(own_rows, wide.at[pl.ds(2 * n_blk, n_blk)], 0, -1, 0, halo_r.at[1])

    live = live_ref[q]
    base = (p - 1) * n_blk
    total_blocks = n_at * n_blk

    def near_id(s):
        return jnp.minimum(lax.rem(nb_ref[q, s] - base + total_blocks, total_blocks), 3 * n_blk - 1)

    near = [near_id(s) for s in range(n_slot)]
    for c in range(3 * n_blk):
        found = jnp.int32(n_slot)
        for s in range(n_slot - 1, -1, -1):
            found = jnp.where((near[s] == c) & (s < live), s, found)
        inv[c] = found

    xpad[...] = jnp.zeros((bs, bs), f32)
    for c in range(n_blk):
        xpad[0:3, :] = pos_ref[:, c * bs : (c + 1) * bs]
        post[c] = xpad[...].T
    own_t[...] = post[q]

    steps = lax.broadcasted_iota(jnp.int32, (n_m, 2 * n_f), 0).astype(f32) - half_m
    gain = jnp.exp(-0.5 * steps * steps)
    for wd, src in ((wd1, f1_ref), (wd2, f2_ref)):
        wd[...] = jnp.concatenate([src[...], src[...]], axis=1) * gain
    xpad[0:n_m, :] = wd2[...]
    wcol[...] = xpad[...].T

    nf[0:3, :] = wave_ref[...].astype(f32)
    depth_side = n_blk * bs / (atom_density * slab_width * slab_height)
    sides = (slab_width * n_at, slab_height, depth_side)
    scales = [2.0 * math.pi / side for side in sides]
    kx, ky, kz = (nf[a : a + 1, :] * scales[a] for a in range(3))
    square = kx * kx + ky * ky + kz * kz
    weight = jnp.exp(-0.5 * spread_square * square) / (square + screen_square) * (2.0 / total_atoms)
    for c in range(k_chunks):
        wtab[c, 0:1, :] = weight[:, c * bs : (c + 1) * bs]

    rows_t = 16
    span = min(n_wave, 512)

    def tables(block):
        def one(step, carry):
            at = pl.multiple_of(step * rows_t, rows_t)
            cols = []
            for a in range(3):
                col = post[block, pl.ds(at, rows_t), a : a + 1] * (1.0 / sides[a])
                cols.append(col - jnp.round(col))
            row = pl.ds(pl.multiple_of(block * bs + at, rows_t), rows_t)
            for start in range(0, n_wave, span):
                lanes = slice(start, start + span)
                u = cols[0] * nf[0:1, lanes] + cols[1] * nf[1:2, lanes] + cols[2] * nf[2:3, lanes]
                sine, cosine = sin_cos_turns(u - jnp.round(u))
                thi[row, lanes], tlo[row, lanes] = split(cosine)
                later = slice(n_wave + start, n_wave + start + span)
                thi[row, later], tlo[row, later] = split(sine)
            return carry

        lax.fori_loop(0, bs // rows_t, one, 0)

    for block in range(n_blk // 2):
        tables(block)

    wait_bytes(own_rows, halo_r.at[0])
    wait_bytes(own_rows, halo_r.at[1])

    rows_g = 32
    centre = cutoff_radius * half_m / (n_m - 1)
    spacing = cutoff_radius / (n_m - 1)
    sharp = 0.5 / spacing ** 2

    def put_values(dest, value, lanes):
        high, low = split(value)
        dest[0:n_f, lanes] = high
        dest[n_f : 2 * n_f, lanes] = low
        dest[2 * n_f : 3 * n_f, lanes] = high
        dest[3 * n_f : 4 * n_f, lanes] = low

    def pairs(s, carry):
        block = near_id(s)
        lanes = pl.ds(pl.multiple_of(s * bs, bs), bs)
        alive = jnp.where(s < live, 1.0, 0.0).astype(f32)
        put_values(zf, wide[block, 0:n_f, :], lanes)
        right = [wide[block, n_f + a : n_f + a + 1, :] for a in range(3)]
        for start in range(0, bs, rows_g):
            rows = slice(start, start + rows_g)
            dx, dy, dz = (own_t[rows, a : a + 1] - right[a] for a in range(3))
            squared = dx * dx + dy * dy + dz * dz + self_offset
            inverse = lax.rsqrt(squared)
            r = squared * inverse
            i = lax.broadcasted_iota(jnp.int32, (rows_g, bs), 0) + start
            j = lax.broadcasted_iota(jnp.int32, (rows_g, bs), 1)
            off = (i - j) * (i - j) + s
            active = jnp.where((r < cutoff_radius) & (off != 0), alive, 0.0)
            r = jnp.minimum(r, cutoff_radius)
            rho = r - centre
            bell = jnp.exp(-sharp * rho * rho)
            tau = jnp.exp((2.0 * sharp * spacing) * rho)
            tin = jnp.exp((-2.0 * sharp * spacing) * rho)
            sine, cosine = sin_cos_turns(r * (0.25 / cutoff_radius))
            cosine = cosine * active
            cut = cosine * cosine
            slope = (-math.pi / cutoff_radius) * sine * cosine
            first = cut * bell
            geo[0, rows, lanes] = dx
            geo[1, rows, lanes] = dy
            geo[2, rows, lanes] = dz
            geo[3, rows, lanes] = tau
            geo[4, rows, lanes] = tin
            geo[5, rows, lanes] = (slope - (2.0 * sharp) * rho * cut) * bell * inverse
            geo[6, rows, lanes] = (2.0 * sharp * spacing) * first * inverse
            term = first
            for m in range(half_m, n_m):
                out = slice(m * bs + start, m * bs + start + rows_g)
                ahi[out, lanes], alo[out, lanes] = split(term)
                term = term * tau
            term = first
            for m in range(half_m - 1, -1, -1):
                term = term * tin
                out = slice(m * bs + start, m * bs + start + rows_g)
                ahi[out, lanes], alo[out, lanes] = split(term)
        return carry

    lax.fori_loop(0, n_slot, pairs, 0)

    group = 4

    def messages(values, wd):
        total = jnp.zeros((bs, 2 * n_f), f32)
        stack = values[0 : 2 * n_f, :]
        for g in range(0, n_m, group):
            rows = slice(g * bs, (g + group) * bs)
            got = dot_nt(ahi[rows, :], stack) + dot_nt(alo[rows, :], stack)
            for m in range(group):
                total = total + got[m * bs : (m + 1) * bs] * wd[g + m : g + m + 1, :]
        flipped = total.T
        return flipped[0:n_f] + flipped[n_f:]

    z_one = wide[n_blk + q, 0:n_f, :] + messages(zf, wd1)
    mine = n_blk + q
    zwide[mine] = z_one
    for dp, dq in near_peers:
        send(zwide.at[mine], zwide.at[(1 - dp) * n_blk + q], 1, dp, dq)
    for block in range(n_blk // 2, n_blk):
        tables(block)
    wait_bytes(zwide.at[pl.ds(0, 3 * n_blk - 1)], rsem.at[1])
    for s in range(n_slot):
        put_values(zz, zwide[near[s]], slice(s * bs, (s + 1) * bs))
    z_two = z_one + messages(zz, wd2)

    qbuf[q] = exact_tn(cw_ref[...], z_two)
    for dq in range(1, n_k):
        send(qbuf.at[q], qbuf.at[q], 2, 0, dq)
    hidden = exact_tn(rin_ref[...], z_two)
    gate = 1.0 / (1.0 + jnp.exp(-hidden))
    bent = gate * (1.0 + hidden * (1.0 - gate))
    short_grad = exact_nn(rin_ref[...] * rout_ref[...], bent)
    wait_bytes(qbuf.at[pl.ds(0, n_k - 1)], rsem.at[2])

    charges = jnp.concatenate([qbuf[c] for c in range(n_blk)], axis=1)
    stacked = jnp.concatenate(split(charges), axis=0)
    got = dot_nn(stacked, thi[...]) + dot_nn(stacked, tlo[...])
    got = got[0:n_q] + got[n_q:]
    for c in range(2 * k_chunks):
        sfb[c] = got[:, c * bs : (c + 1) * bs]
    for d in range(1, n_at):
        send(sfb.at[lax.rem(p + d, n_at)], rsb.at[d - 1], 3, d, 0)
    wait_bytes(rsb, rsem.at[3])
    part = sfb[p]
    for d in range(n_at - 1):
        part = part + rsb[d]
    agb[p] = part * wtab[lax.rem(p, k_chunks), 0:1, :]
    for d in range(1, n_at):
        send(agb.at[p], agb.at[p], 4, d, 0)
    wait_bytes(agb.at[pl.ds(0, n_at - 1)], rsem.at[4])

    for c in range(k_chunks):
        cos_part, sin_part = agb[c], agb[k_chunks + c]
        lanes = slice(c * bs, (c + 1) * bs)
        later = slice(n_wave + c * bs, n_wave + (c + 1) * bs)
        rows = [cos_part] + [sin_part * (nf[a : a + 1, lanes] * scales[a]) for a in range(3)]
        rows2 = [sin_part] + [cos_part * (nf[a : a + 1, lanes] * -scales[a]) for a in range(3)]
        for place, pieces in ((lanes, rows), (later, rows2)):
            for a, piece in enumerate(pieces):
                high, low = split(piece)
                rmat[a * n_q : (a + 1) * n_q, place] = high
                rmat[(4 + a) * n_q : (5 + a) * n_q, place] = low
    got = dot_nt(thi[...], rmat[...]) + dot_nt(tlo[...], rmat[...])
    folded = []
    for c in range(n_blk):
        flipped = got[c * bs : (c + 1) * bs].T
        flipped = flipped[0 : 4 * n_q] + flipped[4 * n_q :]
        cgs[c] = flipped[0:n_q]
        folded.append(flipped)
    for dq in range(1, n_k):
        send(cgs.at[lax.rem(q + dq, n_k)], cgr.at[dq - 1], 5, 0, dq)
    for c in range(n_blk):
        for a in range(3):
            product = qbuf[c] * folded[c][(1 + a) * n_q : (2 + a) * n_q]
            wf[a : a + 1, c * bs : (c + 1) * bs] = jnp.sum(product, axis=0, keepdims=True)
    wait_bytes(cgr, rsem.at[5])
    charge_grad = cgs[q] + cgr[0]
    for dq in range(1, n_k - 1):
        charge_grad = charge_grad + cgr[dq]
    g_two = exact_nn(cw_ref[...], charge_grad) + short_grad

    for m in range(n_m):
        lanes = slice(m * bs, (m + 1) * bs)
        high, low = split(g_two * wcol[0:n_f, m : m + 1])
        gwt[0:n_f, lanes] = high
        gwt[n_f:, lanes] = low
    got = dot_nn(gwt[...], ahi[...]) + dot_nn(gwt[...], alo[...])
    got = got[0:n_f] + got[n_f:]
    for s in range(n_slot):
        tslot[s] = got[:, s * bs : (s + 1) * bs]
    tslot[n_slot] = jnp.zeros((n_f, bs), f32)
    for index, (dp, dq) in enumerate(near_peers):
        block = (1 + dp) * n_blk + lax.rem(q + dq, n_k)
        tsend[index] = tslot[inv[block]]
        send(tsend.at[index], trecv.at[index], 6, dp, dq)

    def pair_sums(grad, wd, values, last):
        twice = jnp.concatenate([grad, grad], axis=0).T
        for m in range(n_m):
            rows = slice(m * bs, (m + 1) * bs)
            high, low = split(twice * wd[m : m + 1, :])
            gw[rows, 0 : 2 * n_f] = high
            gw[rows, 2 * n_f :] = low
        rows_h = 16
        for tile, start in enumerate(range(0, wide_n, 2 * bs)):
            width = min(2 * bs, wide_n - start)
            lanes = slice(start, start + width)
            buf = tile % 2
            bbuf[buf, :, 0:width] = dot_nn(gw[...], values[:, lanes])

            def horner(step, carry):
                at = pl.multiple_of(step * rows_h, rows_h)
                rows = pl.ds(at, rows_h)

                def term(m):
                    here = pl.ds(pl.multiple_of(m * bs + at, rows_h), rows_h)
                    return bbuf[buf, here, 0:width]

                tau = geo[3, rows, lanes]
                up = term(n_m - 1)
                up_d = up
                for m in range(n_m - 2, half_m, -1):
                    up = up * tau + term(m)
                    up_d = up_d * tau + up
                up = up * tau + term(half_m)
                tin = geo[4, rows, lanes]
                down = term(0)
                down_d = down
                for m in range(1, half_m):
                    down = down * tin + term(m)
                    down_d = down_d * tin + down
                zero_sum = up + down * tin
                one_sum = up_d * tau - down_d * tin
                value = geo[5, rows, lanes] * zero_sum + geo[6, rows, lanes] * one_sum
                if last:
                    value = value + qsum[rows, lanes]
                qsum[rows, lanes] = value
                return carry

            lax.fori_loop(0, bs // rows_h, horner, 0)

    pair_sums(g_two, wd2, zz, False)
    wait_bytes(trecv, rsem.at[6])
    g_one = g_two + tslot[0]
    for index in range(len(near_peers)):
        g_one = g_one + trecv[index]
    pair_sums(g_one, wd1, zf, True)

    own = [jnp.zeros((bs, bs), f32) for _ in range(3)]
    for s in range(n_slot):
        lanes = slice(s * bs, (s + 1) * bs)
        value = qsum[:, lanes]
        for a in range(3):
            product = value * geo[a, :, lanes]
            own[a] = own[a] + product
            pg[s, a : a + 1, :] = -jnp.sum(product, axis=0, keepdims=True)
    pg[n_slot, 0:3, :] = jnp.zeros((3, bs), f32)
    for a in range(3):
        pg[0, a : a + 1, :] = pg[0, a : a + 1, :] + jnp.sum(own[a].T, axis=0, keepdims=True)
    fsend[...] = jnp.zeros(fsend.shape, f32)
    for side in range(3):
        for c in range(n_blk):
            lanes = slice(c * bs, (c + 1) * bs)
            value = pg[inv[side * n_blk + c], 0:3, :]
            if side == 1:
                value = value + wf[0:3, lanes]
            fsend[side, 0:3, lanes] = value
    for index, (dp, dq) in enumerate(near_peers):
        send(fsend.at[1 + dp], frecv.at[index], 7, dp, dq)
    wait_bytes(frecv, rsem.at[7])
    force = fsend[1, 0:3, :]
    for index in range(len(near_peers)):
        force = force + frecv[index, 0:3, :]
    out_ref[...] = -force

    wait_bytes(wide.at[pl.ds(0, 2 * n_blk)], ssem.at[0])
    wait_bytes(zwide.at[pl.ds(0, 3 * n_blk - 1)], ssem.at[1])
    wait_bytes(qbuf.at[pl.ds(0, n_k - 1)], ssem.at[2])
    wait_bytes(rsb, ssem.at[3])
    wait_bytes(agb.at[pl.ds(0, n_at - 1)], ssem.at[4])
    wait_bytes(cgr, ssem.at[5])
    wait_bytes(trecv, ssem.at[6])
    wait_bytes(frecv, ssem.at[7])


def body(
    n_at, n_k,
    positions, features, filter_one, filter_two, readout_in, readout_out, charge_weight,
    neighbour_blocks, live_slots, wave_ints,
):
    n_f = features.shape[0]
    n_m = filter_one.shape[0]
    n_q = charge_weight.shape[1]
    n_blk, n_slot = neighbour_blocks.shape
    bs = positions.shape[1] // n_blk
    n_wave = wave_ints.shape[1]
    local = n_blk * bs
    wide_n = n_slot * bs
    near_n = 3 * n_blk - 1
    k_chunks = n_wave // bs
    sizes = (n_at, n_k, n_blk, bs, n_slot, n_f, n_m, n_q, n_wave)
    v = pltpu.VMEM
    scratch = [
        v((3 * n_blk, n_f + 8, bs), f32),
        v((3 * n_blk, n_f, bs), f32),
        v((n_blk, bs, bs), f32),
        v((bs, bs), f32),
        v((bs, bs), f32),
        v((8, n_wave), f32),
        v((k_chunks, 8, bs), f32),
        v((local, 2 * n_wave), bf16),
        v((local, 2 * n_wave), bf16),
        v((n_m * bs, wide_n), bf16),
        v((n_m * bs, wide_n), bf16),
        v((4 * n_f, wide_n), bf16),
        v((4 * n_f, wide_n), bf16),
        v((7, bs, wide_n), f32),
        v((n_m, 2 * n_f), f32),
        v((n_m, 2 * n_f), f32),
        v((bs, bs), f32),
        v((2 * n_f, n_m * bs), bf16),
        v((n_m * bs, 4 * n_f), bf16),
        v((2, n_m * bs, 2 * bs), f32),
        v((bs, wide_n), f32),
        v((n_slot + 1, n_f, bs), f32),
        v((near_n, n_f, bs), f32),
        v((near_n, n_f, bs), f32),
        v((n_k, n_q, bs), f32),
        v((n_at, n_q, bs), f32),
        v((n_at - 1, n_q, bs), f32),
        v((n_at, n_q, bs), f32),
        v((8 * n_q, 2 * n_wave), bf16),
        v((n_blk, n_q, bs), f32),
        v((n_k - 1, n_q, bs), f32),
        v((8, local), f32),
        v((n_slot + 1, 8, bs), f32),
        v((3, 8, local), f32),
        v((near_n, 8, local), f32),
        pltpu.SMEM((3 * n_blk,), jnp.int32),
        pltpu.SemaphoreType.DMA((8,)),
        pltpu.SemaphoreType.DMA((8,)),
        pltpu.SemaphoreType.DMA((2,)),
    ]
    vmem = pl.BlockSpec(memory_space=pltpu.VMEM)
    smem = pl.BlockSpec(memory_space=pltpu.SMEM)
    return pl.pallas_call(
        functools.partial(kernel, sizes),
        out_shape=jax.ShapeDtypeStruct(positions.shape, f32),
        in_specs=[vmem] * 8 + [smem] * 2,
        out_specs=vmem,
        scratch_shapes=scratch,
        compiler_params=pltpu.CompilerParams(
            collective_id=0, has_side_effects=True, vmem_limit_bytes=56 * 2**20
        ),
    )(
        positions, features, filter_one, filter_two, readout_in,
        readout_out.reshape(1, n_f), charge_weight, wave_ints, neighbour_blocks, live_slots,
    )


def solution(mesh):
    in_specs = (
        P(None, "atoms"), P(None, "atoms"), P(), P(), P(), P(), P(),
        P("atoms", None), P("atoms"), P(None, "kvec"),
    )
    return jax.shard_map(
        functools.partial(body, mesh.shape["atoms"], mesh.shape["kvec"]),
        mesh=mesh, in_specs=in_specs, out_specs=P(None, "atoms"), check_vma=False,
    )
```

time: 639 us -> 78.8 us (0.12); the launches traced: 628 us -> 78.6 us
  matrix products: 288 us -> 0 us
  waiting for transfers between devices: 115 us -> 0 us
  other arithmetic: 95.8 us -> 0 us
  Pallas kernels: 0 us -> 75.9 us
  local copies, waits for them, and re-layouts: 42.7 us -> 2.68 us
  loops' own time: 34.9 us -> 0 us
  starting transfers between devices: 18.4 us -> 0 us
  blocking collectives: 18.1 us -> 0 us
  between operations: 14.2 us -> 0.01 us
    dot_general x40 -> x0, matrix products: 288 us -> none  [the longest x20 230 us: block_messages(): jnp.einsum('mij,fj->mfi', radial_terms, values, precision=highest)]
    psum x1 -> x0, waiting for transfers between devices: 110 us -> none  [body(): cosine_sum, sine_sum = lax.psum((cosine_part, sine_part), 'atoms')]
    pallas_call x0 -> x1, Pallas kernels: none -> 75.9 us  [body(): pl.pallas_call(functools.partial(kernel, sizes), out_shape=jax.ShapeDtype...]
    select_n x52 -> x0, other arithmetic: 47.2 us -> none  [the longest x20 45.8 us: radial(): jnp.where(distance < cutoff_radius, 0.5 * (jnp.cos(jnp.pi * distance / cu...]
    another operation x4 -> x0, loops' own time: 34.9 us -> none  [messages(): lax.map(jax.checkpoint(per_block), jnp.arange(block_count, dtype=jnp.int32))]
    mul x12 -> x0, other arithmetic: 19.8 us -> none  [the longest x8 18.3 us: block_messages(): distance = jnp.sqrt(jnp.sum(offset * offset, axis=0) + self_offset)]
    ppermute x8 -> x0, starting transfers between devices: 18.4 us -> none  [the longest x4 9.67 us: from_behind(): return lax.ppermute(block, axis, route)]
    gather x32 -> x0, local copies, waits for them, and re-layouts: 18.3 us -> none  [the longest x16 9.21 us: per_block(): near_pos = jnp.take(pos_blocks, chosen, axis=1)]
  transfers between devices with their start and end apart: 9 -> 0, of which waited for: 4 -> 0; matrix products, arithmetic and copies ran while one was open for 4% -> 0% of each run, Pallas kernels for 0% -> 0%
where the time goes in v1:
time: 78.8 us; the launch traced here: 78.6 us
  Pallas kernels  75.9 us (96%)
  local copies, waits for them, and re-layouts  2.68 us (3%)
    pallas_call x1, Pallas kernels, body(): pl.pallas_call(functools.partial(kernel, sizes), out_shape=jax.ShapeDtype...  75.9 us
    unnamed x2, local copies, waits for them, and re-layouts  2.68 us

profile of v1, /device:TPU:0, one launch (start us, length us, event | category | flops | bytes accessed | tf_op | source)
XLA Modules:
  0.0 78.6 jit_solution(15202277799119620695)
XLA Ops:
  0.0 1.4 %copy.11.cw_ref = f32[64,16]{1,0:T(8,128)} copy(f32[64,16]{0,1:T(8,128)} %param.16) | data formatting | bytes 8192 | tf_op args[6]
  1.4 75.9 %shard_map.100 = f32[3,512]{1,0:T(4,128)} custom-call(f32[3,512]{1,0:T(4,128)} %pos_ref.1, f32[64,512]{1,0:T(8,128)} %feat_ref.1, f32[16,64]{1,0:T(8,128)} %f1_ref.1, f32[16,64]{1,0:T(8,128)} %f2_ref.1, f32[64,64]{1,0:T(8,128)} %rin_ref.1, f32[1,64]{1,0:T(1,128)} %bitcast.1, f32[64,16]{1,0:T(8,128)} %copy.11.cw_ref, s32[3,2048]{1,0:T(4,128)} %wave_ref.1, ...), custom_call_target="tpu_custom_call" | custom-call | tf_op jit(solution)/shard_map/pallas_call | solution.py:496
  77.3 1.3 %copy.13 = f32[3,512]{1,0:T(4,128)} copy(f32[3,512]{1,0:T(4,128)} %shard_map.100) | data formatting | bytes 12288

commit v2 on v1

--- a/solution.py
+++ b/solution.py
@@ -20,6 +20,7 @@
 self_offset = 0.0001
 screen_square = 0.25
 spread_square = 1.0
+n_group = 8
 
 
 def trig_coefficients():
@@ -82,9 +83,9 @@
     pos_ref, feat_ref, f1_ref, f2_ref, rin_ref, rout_ref, cw_ref, wave_ref, nb_ref, live_ref,
     out_ref,
     wide, zwide, post, xpad, own_t, nf, wtab, thi, tlo, ahi, alo, zf, zz, geo,
-    wd1, wd2, wcol, gwt, gw, bbuf, qsum, tslot, tsend, trecv, qbuf, sfb, rsb, agb, rmat,
+    wd1, wd2, wcol, gwt, gw, buf_a, buf_b, qsum, tslot, tsend, trecv, qbuf, sfb, rsb, agb, agpart, rmat,
     cgs, cgr, wf, pg, fsend, frecv, inv,
-    ssem, rsem, halo_r,
+    ssem, rsem, halo_r, group_r, greet_sem,
 ):
     n_at, n_k, n_blk, bs, n_slot, n_f, n_m, n_q, n_wave = sizes
     total_atoms = n_at * n_blk * bs
@@ -92,8 +93,11 @@
     q = lax.axis_index("kvec")
     half_m = n_m // 2
     wide_n = n_slot * bs
+    wide_p = zf.shape[1]
     k_chunks = n_wave // bs
-    near_peers = [(dp, dq) for dp in (-1, 0, 1) for dq in range(n_k) if (dp, dq) != (0, 0)]
+    across = [(0, dq) for dq in range(1, n_k)]
+    beside = [(1, 0), (-1, 0)]
+    near_peers = [(dp, dq) for dq in range(1, n_k) for dp in (1, -1)] + across + beside
 
     def peer(dp, dq):
         return {"atoms": lax.rem(p + dp + n_at, n_at), "kvec": lax.rem(q + dq, n_k)}
@@ -110,9 +114,24 @@
         pltpu.make_async_copy(ref, ref, sem).wait()
 
     barrier = pltpu.get_barrier_semaphore()
-    partners = near_peers + [(d, 0) for d in range(2, n_at - 1)]
+    partners = across + beside
     for dp, dq in partners:
         pl.semaphore_signal(barrier, inc=1, device_id=peer(dp, dq), device_id_type=MESH)
+
+    def greet(index, group):
+        for dp, dq in group:
+            pl.semaphore_signal(
+                greet_sem.at[index], inc=1, device_id=peer(dp, dq), device_id_type=MESH
+            )
+
+    def met(index, group):
+        pl.semaphore_wait(greet_sem.at[index], len(group))
+
+    rounds = []
+    reach = 1
+    while reach < n_at // 2:
+        rounds.append([(reach, 0), (-reach, 0)])
+        reach *= 2
 
     for c in range(n_blk):
         lanes = slice(c * bs, (c + 1) * bs)
@@ -123,6 +142,8 @@
     own_rows = wide.at[pl.ds(n_blk, n_blk)]
     send(own_rows, wide.at[pl.ds(0, n_blk)], 0, 1, 0, halo_r.at[0])
     send(own_rows, wide.at[pl.ds(2 * n_blk, n_blk)], 0, -1, 0, halo_r.at[1])
+    greet(0, across)
+    greet(1, rounds[0])
 
     live = live_ref[q]
     base = (p - 1) * n_blk
@@ -186,9 +207,6 @@
     for block in range(n_blk // 2):
         tables(block)
 
-    wait_bytes(own_rows, halo_r.at[0])
-    wait_bytes(own_rows, halo_r.at[1])
-
     rows_g = 32
     centre = cutoff_radius * half_m / (n_m - 1)
     spacing = cutoff_radius / (n_m - 1)
@@ -201,8 +219,7 @@
         dest[2 * n_f : 3 * n_f, lanes] = high
         dest[3 * n_f : 4 * n_f, lanes] = low
 
-    def pairs(s, carry):
-        block = near_id(s)
+    def pairs(s, block):
         lanes = pl.ds(pl.multiple_of(s * bs, bs), bs)
         alive = jnp.where(s < live, 1.0, 0.0).astype(f32)
         put_values(zf, wide[block, 0:n_f, :], lanes)
@@ -244,36 +261,61 @@
                 term = term * tin
                 out = slice(m * bs + start, m * bs + start + rows_g)
                 ahi[out, lanes], alo[out, lanes] = split(term)
+
+    def near_pairs(s, carry):
+        pairs(s, near_id(s))
         return carry
 
-    lax.fori_loop(0, n_slot, pairs, 0)
-
     group = 4
 
-    def messages(values, wd):
-        total = jnp.zeros((bs, 2 * n_f), f32)
-        stack = values[0 : 2 * n_f, :]
+    def messages(values, wd, lanes, total):
+        stack = values[0 : 2 * n_f, lanes]
         for g in range(0, n_m, group):
             rows = slice(g * bs, (g + group) * bs)
-            got = dot_nt(ahi[rows, :], stack) + dot_nt(alo[rows, :], stack)
+            got = dot_nt(ahi[rows, lanes], stack) + dot_nt(alo[rows, lanes], stack)
             for m in range(group):
                 total = total + got[m * bs : (m + 1) * bs] * wd[g + m : g + m + 1, :]
+        return total
+
+    def upright(total):
         flipped = total.T
         return flipped[0:n_f] + flipped[n_f:]
 
-    z_one = wide[n_blk + q, 0:n_f, :] + messages(zf, wd1)
+    first_lanes, later_lanes = slice(0, bs), slice(bs, wide_n)
+    nothing = jnp.zeros((bs, 2 * n_f), f32)
     mine = n_blk + q
+    if wide_p > wide_n:
+        spare = slice(wide_n, wide_p)
+        for values in (zf, zz):
+            values[:, spare] = jnp.zeros((4 * n_f, wide_p - wide_n), bf16)
+        for index in range(3, 7):
+            geo[index, :, spare] = jnp.zeros((bs, wide_p - wide_n), f32)
+    pairs(0, mine)
+    total = messages(zf, wd1, first_lanes, nothing)
+    met(1, rounds[0])
+    greet(2, rounds[1])
+    wait_bytes(own_rows, halo_r.at[0])
+    wait_bytes(own_rows, halo_r.at[1])
+    lax.fori_loop(1, n_slot, near_pairs, 0)
+    met(2, rounds[1])
+    greet(3, rounds[2])
+    z_one = wide[mine, 0:n_f, :] + upright(messages(zf, wd1, later_lanes, total))
     zwide[mine] = z_one
+    met(0, across)
     for dp, dq in near_peers:
         send(zwide.at[mine], zwide.at[(1 - dp) * n_blk + q], 1, dp, dq)
     for block in range(n_blk // 2, n_blk):
         tables(block)
+    met(3, rounds[2])
+    greet(4, rounds[3])
+    put_values(zz, z_one, first_lanes)
+    total = messages(zz, wd2, first_lanes, nothing)
     wait_bytes(zwide.at[pl.ds(0, 3 * n_blk - 1)], rsem.at[1])
-    for s in range(n_slot):
+    for s in range(1, n_slot):
         put_values(zz, zwide[near[s]], slice(s * bs, (s + 1) * bs))
-    z_two = z_one + messages(zz, wd2)
-
-    qbuf[q] = exact_tn(cw_ref[...], z_two)
+    z_two = z_one + upright(messages(zz, wd2, later_lanes, total))
+
+    qbuf[q] = exact_nn(cw_ref[...], z_two)
     for dq in range(1, n_k):
         send(qbuf.at[q], qbuf.at[q], 2, 0, dq)
     hidden = exact_tn(rin_ref[...], z_two)
@@ -284,33 +326,57 @@
 
     charges = jnp.concatenate([qbuf[c] for c in range(n_blk)], axis=1)
     stacked = jnp.concatenate(split(charges), axis=0)
-    got = dot_nn(stacked, thi[...]) + dot_nn(stacked, tlo[...])
-    got = got[0:n_q] + got[n_q:]
-    for c in range(2 * k_chunks):
-        sfb[c] = got[:, c * bs : (c + 1) * bs]
-    for d in range(1, n_at):
-        send(sfb.at[lax.rem(p + d, n_at)], rsb.at[d - 1], 3, d, 0)
+    met(4, rounds[3])
+    pair_k = n_group // 2
+    span_k = pair_k * bs
+    groups = n_at // n_group
+    own_group, own_place = p // n_group, lax.rem(p, n_group)
+    for step in range(groups):
+        this = lax.rem(own_group + step, groups)
+        for kind in range(2):
+            lanes = pl.ds(pl.multiple_of(kind * n_wave + this * span_k, bs), span_k)
+            got = dot_nn(stacked, thi[:, lanes]) + dot_nn(stacked, tlo[:, lanes])
+            got = got[0:n_q] + got[n_q:]
+            for c in range(pair_k):
+                sfb[this * n_group + 2 * c + kind] = got[:, c * bs : (c + 1) * bs]
+        for c in range(1 if step == 0 else 0, n_group):
+            place = lax.rem(own_place + c, n_group)
+            target = this * n_group + place
+            ahead = lax.rem(target - p + n_at, n_at)
+            send(sfb.at[target], rsb.at[ahead - 1], 3, ahead, 0)
     wait_bytes(rsb, rsem.at[3])
     part = sfb[p]
     for d in range(n_at - 1):
         part = part + rsb[d]
-    agb[p] = part * wtab[lax.rem(p, k_chunks), 0:1, :]
-    for d in range(1, n_at):
-        send(agb.at[p], agb.at[p], 4, d, 0)
-    wait_bytes(agb.at[pl.ds(0, n_at - 1)], rsem.at[4])
-
-    for c in range(k_chunks):
-        cos_part, sin_part = agb[c], agb[k_chunks + c]
-        lanes = slice(c * bs, (c + 1) * bs)
-        later = slice(n_wave + c * bs, n_wave + (c + 1) * bs)
-        rows = [cos_part] + [sin_part * (nf[a : a + 1, lanes] * scales[a]) for a in range(3)]
-        rows2 = [sin_part] + [cos_part * (nf[a : a + 1, lanes] * -scales[a]) for a in range(3)]
-        for place, pieces in ((lanes, rows), (later, rows2)):
-            for a, piece in enumerate(pieces):
-                high, low = split(piece)
-                rmat[a * n_q : (a + 1) * n_q, place] = high
-                rmat[(4 + a) * n_q : (5 + a) * n_q, place] = low
-    got = dot_nt(thi[...], rmat[...]) + dot_nt(tlo[...], rmat[...])
+    agpart[...] = part * wtab[p // 2, 0:1, :]
+    for d in range(1, n_at // 2 + 1):
+        for dp in sorted({d, n_at - d}):
+            send(agpart, agb.at[p], 4, dp, 0, group_r.at[own_group])
+    keep = pltpu.make_async_copy(agpart, agb.at[p], group_r.at[own_group])
+    keep.start()
+
+    total = jnp.zeros((n_blk * bs, 8 * n_q), f32)
+    for step in range(groups):
+        this = lax.rem(own_group + step, groups)
+        wait_bytes(agb.at[pl.ds(0, n_group)], group_r.at[this])
+        for c in range(pair_k):
+            at = pl.multiple_of(this * span_k + c * bs, bs)
+            cos_part = agb[this * n_group + 2 * c]
+            sin_part = agb[this * n_group + 2 * c + 1]
+            ks = [nf[a : a + 1, pl.ds(at, bs)] * scales[a] for a in range(3)]
+            rows = [cos_part] + [sin_part * k for k in ks]
+            rows2 = [sin_part] + [cos_part * -k for k in ks]
+            for kind, pieces in ((0, rows), (1, rows2)):
+                place = slice(kind * span_k + c * bs, kind * span_k + (c + 1) * bs)
+                for a, piece in enumerate(pieces):
+                    high, low = split(piece)
+                    rmat[step, a * n_q : (a + 1) * n_q, place] = high
+                    rmat[step, (4 + a) * n_q : (5 + a) * n_q, place] = low
+        for kind in range(2):
+            lanes = pl.ds(pl.multiple_of(kind * n_wave + this * span_k, bs), span_k)
+            right = rmat[step, :, kind * span_k : (kind + 1) * span_k]
+            total = total + dot_nt(thi[:, lanes], right) + dot_nt(tlo[:, lanes], right)
+    got = total
     folded = []
     for c in range(n_blk):
         flipped = got[c * bs : (c + 1) * bs].T
@@ -322,12 +388,13 @@
     for c in range(n_blk):
         for a in range(3):
             product = qbuf[c] * folded[c][(1 + a) * n_q : (2 + a) * n_q]
-            wf[a : a + 1, c * bs : (c + 1) * bs] = jnp.sum(product, axis=0, keepdims=True)
+            row = a * n_blk + c
+            wf[row : row + 1, :] = jnp.sum(product, axis=0, keepdims=True)
     wait_bytes(cgr, rsem.at[5])
     charge_grad = cgs[q] + cgr[0]
     for dq in range(1, n_k - 1):
         charge_grad = charge_grad + cgr[dq]
-    g_two = exact_nn(cw_ref[...], charge_grad) + short_grad
+    g_two = exact_tn(cw_ref[...], charge_grad) + short_grad
 
     for m in range(n_m):
         lanes = slice(m * bs, (m + 1) * bs)
@@ -344,50 +411,69 @@
         tsend[index] = tslot[inv[block]]
         send(tsend.at[index], trecv.at[index], 6, dp, dq)
 
+    rows_c = 32
+    rows_h = 16
+    tile = 2 * bs
+    tiles = wide_p // tile
+    steps_p = bs // rows_c * tiles
+
     def pair_sums(grad, wd, values, last):
         twice = jnp.concatenate([grad, grad], axis=0).T
-        for m in range(n_m):
-            rows = slice(m * bs, (m + 1) * bs)
-            high, low = split(twice * wd[m : m + 1, :])
-            gw[rows, 0 : 2 * n_f] = high
-            gw[rows, 2 * n_f :] = low
-        rows_h = 16
-        for tile, start in enumerate(range(0, wide_n, 2 * bs)):
-            width = min(2 * bs, wide_n - start)
-            lanes = slice(start, start + width)
-            buf = tile % 2
-            bbuf[buf, :, 0:width] = dot_nn(gw[...], values[:, lanes])
-
-            def horner(step, carry):
-                at = pl.multiple_of(step * rows_h, rows_h)
-                rows = pl.ds(at, rows_h)
+        for chunk in range(bs // rows_c):
+            for m in range(n_m):
+                start = (chunk * n_m + m) * rows_c
+                rows = slice(start, start + rows_c)
+                high, low = split(twice[chunk * rows_c : (chunk + 1) * rows_c] * wd[m : m + 1, :])
+                gw[rows, 0 : 2 * n_f] = high
+                gw[rows, 2 * n_f :] = low
+
+        def product(step, buf):
+            height = n_m * rows_c
+            rows = pl.ds(pl.multiple_of(step // tiles * height, height), height)
+            lanes = pl.ds(pl.multiple_of(lax.rem(step, tiles) * tile, tile), tile)
+            buf[...] = dot_nn(gw[rows, :], values[:, lanes])
+
+        def horner(step, buf):
+            lanes = pl.ds(pl.multiple_of(lax.rem(step, tiles) * tile, tile), tile)
+            for part in range(0, rows_c, rows_h):
+                rows = pl.ds(pl.multiple_of(step // tiles * rows_c + part, rows_h), rows_h)
 
                 def term(m):
-                    here = pl.ds(pl.multiple_of(m * bs + at, rows_h), rows_h)
-                    return bbuf[buf, here, 0:width]
+                    return buf[m * rows_c + part : m * rows_c + part + rows_h, :]
 
                 tau = geo[3, rows, lanes]
+                tin = geo[4, rows, lanes]
                 up = term(n_m - 1)
                 up_d = up
-                for m in range(n_m - 2, half_m, -1):
-                    up = up * tau + term(m)
-                    up_d = up_d * tau + up
-                up = up * tau + term(half_m)
-                tin = geo[4, rows, lanes]
                 down = term(0)
                 down_d = down
                 for m in range(1, half_m):
                     down = down * tin + term(m)
                     down_d = down_d * tin + down
+                    if m < half_m - 1:
+                        up = up * tau + term(n_m - 1 - m)
+                        up_d = up_d * tau + up
+                up = up * tau + term(half_m)
                 zero_sum = up + down * tin
                 one_sum = up_d * tau - down_d * tin
                 value = geo[5, rows, lanes] * zero_sum + geo[6, rows, lanes] * one_sum
                 if last:
                     value = value + qsum[rows, lanes]
                 qsum[rows, lanes] = value
-                return carry
-
-            lax.fori_loop(0, bs // rows_h, horner, 0)
+
+        def both(turn, carry):
+            step = 2 * turn
+            product(step + 1, buf_b)
+            horner(step, buf_a)
+            product(step + 2, buf_a)
+            horner(step + 1, buf_b)
+            return carry
+
+        product(0, buf_a)
+        lax.fori_loop(0, steps_p // 2 - 1, both, 0)
+        product(steps_p - 1, buf_b)
+        horner(steps_p - 2, buf_a)
+        horner(steps_p - 1, buf_b)
 
     pair_sums(g_two, wd2, zz, False)
     wait_bytes(trecv, rsem.at[6])
@@ -410,18 +496,23 @@
     fsend[...] = jnp.zeros(fsend.shape, f32)
     for side in range(3):
         for c in range(n_blk):
-            lanes = slice(c * bs, (c + 1) * bs)
             value = pg[inv[side * n_blk + c], 0:3, :]
-            if side == 1:
-                value = value + wf[0:3, lanes]
-            fsend[side, 0:3, lanes] = value
+            for a in range(3):
+                row = a * n_blk + c
+                piece = value[a : a + 1]
+                if side == 1:
+                    piece = piece + wf[row : row + 1, :]
+                fsend[side, row : row + 1, :] = piece
     for index, (dp, dq) in enumerate(near_peers):
         send(fsend.at[1 + dp], frecv.at[index], 7, dp, dq)
     wait_bytes(frecv, rsem.at[7])
-    force = fsend[1, 0:3, :]
+    force = fsend[1]
     for index in range(len(near_peers)):
-        force = force + frecv[index, 0:3, :]
-    out_ref[...] = -force
+        force = force + frecv[index]
+    for a in range(3):
+        for c in range(n_blk):
+            row = a * n_blk + c
+            out_ref[a : a + 1, c * bs : (c + 1) * bs] = -force[row : row + 1]
 
     wait_bytes(wide.at[pl.ds(0, 2 * n_blk)], ssem.at[0])
     wait_bytes(zwide.at[pl.ds(0, 3 * n_blk - 1)], ssem.at[1])
@@ -446,6 +537,7 @@
     n_wave = wave_ints.shape[1]
     local = n_blk * bs
     wide_n = n_slot * bs
+    wide_p = (n_slot + n_slot % 2) * bs
     near_n = 3 * n_blk - 1
     k_chunks = n_wave // bs
     sizes = (n_at, n_k, n_blk, bs, n_slot, n_f, n_m, n_q, n_wave)
@@ -462,16 +554,17 @@
         v((local, 2 * n_wave), bf16),
         v((n_m * bs, wide_n), bf16),
         v((n_m * bs, wide_n), bf16),
-        v((4 * n_f, wide_n), bf16),
-        v((4 * n_f, wide_n), bf16),
-        v((7, bs, wide_n), f32),
+        v((4 * n_f, wide_p), bf16),
+        v((4 * n_f, wide_p), bf16),
+        v((7, bs, wide_p), f32),
         v((n_m, 2 * n_f), f32),
         v((n_m, 2 * n_f), f32),
         v((bs, bs), f32),
         v((2 * n_f, n_m * bs), bf16),
         v((n_m * bs, 4 * n_f), bf16),
-        v((2, n_m * bs, 2 * bs), f32),
-        v((bs, wide_n), f32),
+        v((n_m * 32, 2 * bs), f32),
+        v((n_m * 32, 2 * bs), f32),
+        v((bs, wide_p), f32),
         v((n_slot + 1, n_f, bs), f32),
         v((near_n, n_f, bs), f32),
         v((near_n, n_f, bs), f32),
@@ -479,17 +572,20 @@
         v((n_at, n_q, bs), f32),
         v((n_at - 1, n_q, bs), f32),
         v((n_at, n_q, bs), f32),
-        v((8 * n_q, 2 * n_wave), bf16),
+        v((n_q, bs), f32),
+        v((n_at // n_group, 8 * n_q, n_group * bs), bf16),
         v((n_blk, n_q, bs), f32),
         v((n_k - 1, n_q, bs), f32),
-        v((8, local), f32),
+        v((16, bs), f32),
         v((n_slot + 1, 8, bs), f32),
-        v((3, 8, local), f32),
-        v((near_n, 8, local), f32),
+        v((3, 16, bs), f32),
+        v((near_n, 16, bs), f32),
         pltpu.SMEM((3 * n_blk,), jnp.int32),
         pltpu.SemaphoreType.DMA((8,)),
         pltpu.SemaphoreType.DMA((8,)),
         pltpu.SemaphoreType.DMA((2,)),
+        pltpu.SemaphoreType.DMA((n_at // n_group,)),
+        pltpu.SemaphoreType.REGULAR((5,)),
     ]
     vmem = pl.BlockSpec(memory_space=pltpu.VMEM)
     smem = pl.BlockSpec(memory_space=pltpu.SMEM)
@@ -504,7 +600,7 @@
         ),
     )(
         positions, features, filter_one, filter_two, readout_in,
-        readout_out.reshape(1, n_f), charge_weight, wave_ints, neighbour_blocks, live_slots,
+        readout_out.reshape(1, n_f), charge_weight.T, wave_ints, neighbour_blocks, live_slots,
     )
 
 

time: 78.8 us -> 70.8 us (0.90)
  Pallas kernels: 75.9 us -> 69.3 us
  local copies, waits for them, and re-layouts: 2.68 us -> 1.3 us
    pallas_call x1, Pallas kernels: 75.9 us -> 69.3 us  [body(): pl.pallas_call(functools.partial(kernel, sizes), out_shape=jax.ShapeDtype...]
    unnamed x2 -> x1, local copies, waits for them, and re-layouts: 2.68 us -> 1.3 us
where the time goes in v2:
time: 70.8 us; the launch traced here: 70.6 us
  Pallas kernels  69.3 us (98%)
  local copies, waits for them, and re-layouts  1.3 us (2%)
    pallas_call x1, Pallas kernels, body(): pl.pallas_call(functools.partial(kernel, sizes), out_shape=jax.ShapeDtype...  69.3 us

profile of v2, /device:TPU:0, one launch (start us, length us, event | category | flops | bytes accessed | tf_op | source)
XLA Modules:
  0.0 70.6 jit_solution(1585214068684565684)
XLA Ops:
  0.0 69.3 %shard_map.100 = f32[3,512]{1,0:T(4,128)} custom-call(f32[3,512]{1,0:T(4,128)} %pos_ref.1, f32[64,512]{1,0:T(8,128)} %feat_ref.1, f32[16,64]{1,0:T(8,128)} %f1_ref.1, f32[16,64]{1,0:T(8,128)} %f2_ref.1, f32[64,64]{1,0:T(8,128)} %rin_ref.1, f32[1,64]{1,0:T(1,128)} %bitcast.3, f32[16,64]{1,0:T(8,128)} %bitcast.2, s32[3,2048]{1,0:T(4,128)} %wave_ref.1, ...), custom_call_target="tpu_custom_call" | custom-call | tf_op jit(solution)/shard_map/pallas_call | solution.py:592
  69.3 1.3 %copy.12 = f32[3,512]{1,0:T(4,128)} copy(f32[3,512]{1,0:T(4,128)} %shard_map.100) | data formatting | bytes 12288

commit v3 on v2

--- a/solution.py
+++ b/solution.py
@@ -58,10 +58,6 @@
     return high, (x - high.astype(f32)).astype(bf16)
 
 
-def dot_nt(a, b):
-    return lax.dot_general(a, b, (((1,), (1,)), ((), ())), preferred_element_type=f32)
-
-
 def dot_nn(a, b):
     return lax.dot_general(a, b, (((1,), (0,)), ((), ())), preferred_element_type=f32)
 
@@ -82,8 +78,8 @@
     sizes,
     pos_ref, feat_ref, f1_ref, f2_ref, rin_ref, rout_ref, cw_ref, wave_ref, nb_ref, live_ref,
     out_ref,
-    wide, zwide, post, xpad, own_t, nf, wtab, thi, tlo, ahi, alo, zf, zz, geo,
-    wd1, wd2, wcol, gwt, gw, buf_a, buf_b, qsum, tslot, tsend, trecv, qbuf, sfb, rsb, agb, agpart, rmat,
+    wide, zwide, post, xpad, own_t, nf, wtab, thi, tlo, vhi, vlo, ahi, alo, uhi, ulo, zf, zz, geo,
+    wd1, wd2, wcol1, wcol2, gwt, gw, buf_a, buf_b, qsum, tslot, tsend, trecv, qbuf, sfb, rsb, agb, agpart, rmat,
     cgs, cgr, wf, pg, fsend, frecv, inv,
     ssem, rsem, halo_r, group_r, greet_sem,
 ):
@@ -146,6 +142,7 @@
     greet(1, rounds[0])
 
     live = live_ref[q]
+    mine = n_blk + q
     base = (p - 1) * n_blk
     total_blocks = n_at * n_blk
 
@@ -169,9 +166,11 @@
     gain = jnp.exp(-0.5 * steps * steps)
     for wd, src in ((wd1, f1_ref), (wd2, f2_ref)):
         wd[...] = jnp.concatenate([src[...], src[...]], axis=1) * gain
-    xpad[0:n_m, :] = wd2[...]
-    wcol[...] = xpad[...].T
-
+    for wcol, wd in ((wcol1, wd1), (wcol2, wd2)):
+        xpad[0:n_m, :] = wd[...]
+        wcol[...] = xpad[...].T
+
+    nf[...] = jnp.zeros(nf.shape, f32)
     nf[0:3, :] = wave_ref[...].astype(f32)
     depth_side = n_blk * bs / (atom_density * slab_width * slab_height)
     sides = (slab_width * n_at, slab_height, depth_side)
@@ -219,29 +218,59 @@
         dest[2 * n_f : 3 * n_f, lanes] = high
         dest[3 * n_f : 4 * n_f, lanes] = low
 
+    def shape(dx, dy, dz, start, s, alive):
+        squared = dx * dx + dy * dy + dz * dz + self_offset
+        inverse = lax.rsqrt(squared)
+        r = squared * inverse
+        i = lax.broadcasted_iota(jnp.int32, (rows_g, bs), 0) + start
+        j = lax.broadcasted_iota(jnp.int32, (rows_g, bs), 1)
+        off = (i - j) * (i - j) + s
+        active = jnp.where((r < cutoff_radius) & (off != 0), alive, 0.0)
+        r = jnp.minimum(r, cutoff_radius)
+        rho = r - centre
+        bell = jnp.exp(-sharp * rho * rho)
+        tau = jnp.exp((2.0 * sharp * spacing) * rho)
+        tin = jnp.exp((-2.0 * sharp * spacing) * rho)
+        sine, cosine = sin_cos_turns(r * (0.25 / cutoff_radius))
+        cosine = cosine * active
+        return active, inverse, rho, bell, tau, tin, sine, cosine, cosine * cosine
+
+    def upright_pairs(s, block):
+        lanes = pl.ds(pl.multiple_of(s * bs, bs), bs)
+        alive = jnp.where(s < live, 1.0, 0.0).astype(f32)
+        put_values(zf, wide[block, 0:n_f, :], lanes)
+        left = wide[block, n_f : n_f + 8, :].T
+        right = [wide[mine, n_f + a : n_f + a + 1, :] for a in range(3)]
+        for start in range(0, bs, rows_g):
+            rows = slice(start, start + rows_g)
+            dx, dy, dz = (left[rows, a : a + 1] - right[a] for a in range(3))
+            shaped = shape(dx, dy, dz, start, s, alive)
+            bell, tau, tin, cut = shaped[3], shaped[4], shaped[5], shaped[8]
+            first = cut * bell
+            out = pl.ds(pl.multiple_of(s * bs + start, rows_g), rows_g)
+            term = first
+            for m in range(half_m, n_m):
+                place = slice(m * bs, (m + 1) * bs)
+                uhi[out, place], ulo[out, place] = split(term)
+                term = term * tau
+            term = first
+            for m in range(half_m - 1, -1, -1):
+                term = term * tin
+                place = slice(m * bs, (m + 1) * bs)
+                uhi[out, place], ulo[out, place] = split(term)
+
+    def near_upright(s, carry):
+        upright_pairs(s, near_id(s))
+        return carry
+
     def pairs(s, block):
         lanes = pl.ds(pl.multiple_of(s * bs, bs), bs)
         alive = jnp.where(s < live, 1.0, 0.0).astype(f32)
-        put_values(zf, wide[block, 0:n_f, :], lanes)
         right = [wide[block, n_f + a : n_f + a + 1, :] for a in range(3)]
         for start in range(0, bs, rows_g):
             rows = slice(start, start + rows_g)
             dx, dy, dz = (own_t[rows, a : a + 1] - right[a] for a in range(3))
-            squared = dx * dx + dy * dy + dz * dz + self_offset
-            inverse = lax.rsqrt(squared)
-            r = squared * inverse
-            i = lax.broadcasted_iota(jnp.int32, (rows_g, bs), 0) + start
-            j = lax.broadcasted_iota(jnp.int32, (rows_g, bs), 1)
-            off = (i - j) * (i - j) + s
-            active = jnp.where((r < cutoff_radius) & (off != 0), alive, 0.0)
-            r = jnp.minimum(r, cutoff_radius)
-            rho = r - centre
-            bell = jnp.exp(-sharp * rho * rho)
-            tau = jnp.exp((2.0 * sharp * spacing) * rho)
-            tin = jnp.exp((-2.0 * sharp * spacing) * rho)
-            sine, cosine = sin_cos_turns(r * (0.25 / cutoff_radius))
-            cosine = cosine * active
-            cut = cosine * cosine
+            active, inverse, rho, bell, tau, tin, sine, cosine, cut = shape(dx, dy, dz, start, s, alive)
             slope = (-math.pi / cutoff_radius) * sine * cosine
             first = cut * bell
             geo[0, rows, lanes] = dx
@@ -268,38 +297,34 @@
 
     group = 4
 
-    def messages(values, wd, lanes, total):
+    def messages(values, wcol, lanes, total):
         stack = values[0 : 2 * n_f, lanes]
         for g in range(0, n_m, group):
-            rows = slice(g * bs, (g + group) * bs)
-            got = dot_nt(ahi[rows, lanes], stack) + dot_nt(alo[rows, lanes], stack)
+            place = slice(g * bs, (g + group) * bs)
+            got = dot_nn(stack, uhi[lanes, place]) + dot_nn(stack, ulo[lanes, place])
+            got = got[0:n_f] + got[n_f:]
             for m in range(group):
-                total = total + got[m * bs : (m + 1) * bs] * wd[g + m : g + m + 1, :]
+                weights = wcol[0:n_f, g + m : g + m + 1]
+                total = total + got[:, m * bs : (m + 1) * bs] * weights
         return total
 
-    def upright(total):
-        flipped = total.T
-        return flipped[0:n_f] + flipped[n_f:]
-
     first_lanes, later_lanes = slice(0, bs), slice(bs, wide_n)
-    nothing = jnp.zeros((bs, 2 * n_f), f32)
-    mine = n_blk + q
     if wide_p > wide_n:
         spare = slice(wide_n, wide_p)
         for values in (zf, zz):
             values[:, spare] = jnp.zeros((4 * n_f, wide_p - wide_n), bf16)
         for index in range(3, 7):
             geo[index, :, spare] = jnp.zeros((bs, wide_p - wide_n), f32)
-    pairs(0, mine)
-    total = messages(zf, wd1, first_lanes, nothing)
+    upright_pairs(0, mine)
+    total = messages(zf, wcol1, first_lanes, wide[mine, 0:n_f, :])
     met(1, rounds[0])
     greet(2, rounds[1])
     wait_bytes(own_rows, halo_r.at[0])
     wait_bytes(own_rows, halo_r.at[1])
-    lax.fori_loop(1, n_slot, near_pairs, 0)
+    lax.fori_loop(1, n_slot, near_upright, 0)
     met(2, rounds[1])
     greet(3, rounds[2])
-    z_one = wide[mine, 0:n_f, :] + upright(messages(zf, wd1, later_lanes, total))
+    z_one = messages(zf, wcol1, later_lanes, total)
     zwide[mine] = z_one
     met(0, across)
     for dp, dq in near_peers:
@@ -309,11 +334,11 @@
     met(3, rounds[2])
     greet(4, rounds[3])
     put_values(zz, z_one, first_lanes)
-    total = messages(zz, wd2, first_lanes, nothing)
+    total = messages(zz, wcol2, first_lanes, z_one)
     wait_bytes(zwide.at[pl.ds(0, 3 * n_blk - 1)], rsem.at[1])
     for s in range(1, n_slot):
         put_values(zz, zwide[near[s]], slice(s * bs, (s + 1) * bs))
-    z_two = z_one + upright(messages(zz, wd2, later_lanes, total))
+    z_two = messages(zz, wcol2, later_lanes, total)
 
     qbuf[q] = exact_nn(cw_ref[...], z_two)
     for dq in range(1, n_k):
@@ -344,6 +369,8 @@
             target = this * n_group + place
             ahead = lax.rem(target - p + n_at, n_at)
             send(sfb.at[target], rsb.at[ahead - 1], 3, ahead, 0)
+    pairs(0, mine)
+    lax.fori_loop(1, n_slot, near_pairs, 0)
     wait_bytes(rsb, rsem.at[3])
     part = sfb[p]
     for d in range(n_at - 1):
@@ -355,7 +382,27 @@
     keep = pltpu.make_async_copy(agpart, agb.at[p], group_r.at[own_group])
     keep.start()
 
-    total = jnp.zeros((n_blk * bs, 8 * n_q), f32)
+    places = []
+    for a in range(3):
+        turns = pos_ref[a : a + 1, :] * (1.0 / sides[a])
+        places.append(turns - jnp.round(turns))
+
+    def upright_tables(chunk, carry):
+        at = pl.multiple_of(chunk * bs, bs)
+        down = nf[:, pl.ds(at, bs)].T
+        for start in range(0, bs, rows_t):
+            ks = [down[start : start + rows_t, a : a + 1] for a in range(3)]
+            u = ks[0] * places[0] + ks[1] * places[1] + ks[2] * places[2]
+            sine, cosine = sin_cos_turns(u - jnp.round(u))
+            row = pl.ds(pl.multiple_of(at + start, rows_t), rows_t)
+            vhi[row, :], vlo[row, :] = split(cosine)
+            row = pl.ds(pl.multiple_of(n_wave + at + start, rows_t), rows_t)
+            vhi[row, :], vlo[row, :] = split(sine)
+        return carry
+
+    lax.fori_loop(0, k_chunks, upright_tables, 0)
+
+    total = jnp.zeros((8 * n_q, n_blk * bs), f32)
     for step in range(groups):
         this = lax.rem(own_group + step, groups)
         wait_bytes(agb.at[pl.ds(0, n_group)], group_r.at[this])
@@ -375,14 +422,12 @@
         for kind in range(2):
             lanes = pl.ds(pl.multiple_of(kind * n_wave + this * span_k, bs), span_k)
             right = rmat[step, :, kind * span_k : (kind + 1) * span_k]
-            total = total + dot_nt(thi[:, lanes], right) + dot_nt(tlo[:, lanes], right)
-    got = total
+            total = total + dot_nn(right, vhi[lanes, :]) + dot_nn(right, vlo[lanes, :])
+    total = total[0 : 4 * n_q] + total[4 * n_q :]
     folded = []
     for c in range(n_blk):
-        flipped = got[c * bs : (c + 1) * bs].T
-        flipped = flipped[0 : 4 * n_q] + flipped[4 * n_q :]
-        cgs[c] = flipped[0:n_q]
-        folded.append(flipped)
+        folded.append(total[:, c * bs : (c + 1) * bs])
+        cgs[c] = folded[c][0:n_q]
     for dq in range(1, n_k):
         send(cgs.at[lax.rem(q + dq, n_k)], cgr.at[dq - 1], 5, 0, dq)
     for c in range(n_blk):
@@ -398,7 +443,7 @@
 
     for m in range(n_m):
         lanes = slice(m * bs, (m + 1) * bs)
-        high, low = split(g_two * wcol[0:n_f, m : m + 1])
+        high, low = split(g_two * wcol2[0:n_f, m : m + 1])
         gwt[0:n_f, lanes] = high
         gwt[n_f:, lanes] = low
     got = dot_nn(gwt[...], ahi[...]) + dot_nn(gwt[...], alo[...])
@@ -552,13 +597,18 @@
         v((k_chunks, 8, bs), f32),
         v((local, 2 * n_wave), bf16),
         v((local, 2 * n_wave), bf16),
+        v((2 * n_wave, local), bf16),
+        v((2 * n_wave, local), bf16),
         v((n_m * bs, wide_n), bf16),
         v((n_m * bs, wide_n), bf16),
+        v((wide_n, n_m * bs), bf16),
+        v((wide_n, n_m * bs), bf16),
         v((4 * n_f, wide_p), bf16),
         v((4 * n_f, wide_p), bf16),
         v((7, bs, wide_p), f32),
         v((n_m, 2 * n_f), f32),
         v((n_m, 2 * n_f), f32),
+        v((bs, bs), f32),
         v((bs, bs), f32),
         v((2 * n_f, n_m * bs), bf16),
         v((n_m * bs, 4 * n_f), bf16),

time: 70.8 us -> 67.3 us (0.951)
  Pallas kernels: 69.3 us -> 65.8 us
    pallas_call x1, Pallas kernels: 69.3 us -> 65.8 us  [body(): pl.pallas_call(functools.partial(kernel, sizes), out_shape=jax.ShapeDtype...]
where the time goes in v3:
time: 67.3 us; the launch traced here: 67.1 us
  Pallas kernels  65.8 us (98%)
  local copies, waits for them, and re-layouts  1.3 us (2%)
    pallas_call x1, Pallas kernels, body(): pl.pallas_call(functools.partial(kernel, sizes), out_shape=jax.ShapeDtype...  65.8 us

profile of v3, /device:TPU:0, one launch (start us, length us, event | category | flops | bytes accessed | tf_op | source)
XLA Modules:
  0.0 67.1 jit_solution(8882792009492548938)
XLA Ops:
  0.0 65.8 %shard_map.100 = f32[3,512]{1,0:T(4,128)} custom-call(f32[3,512]{1,0:T(4,128)} %pos_ref.1, f32[64,512]{1,0:T(8,128)} %feat_ref.1, f32[16,64]{1,0:T(8,128)} %f1_ref.1, f32[16,64]{1,0:T(8,128)} %f2_ref.1, f32[64,64]{1,0:T(8,128)} %rin_ref.1, f32[1,64]{1,0:T(1,128)} %bitcast.3, f32[16,64]{1,0:T(8,128)} %bitcast.2, s32[3,2048]{1,0:T(4,128)} %wave_ref.1, ...), custom_call_target="tpu_custom_call" | custom-call | tf_op jit(solution)/shard_map/pallas_call | solution.py:642
  65.8 1.3 %copy.12 = f32[3,512]{1,0:T(4,128)} copy(f32[3,512]{1,0:T(4,128)} %shard_map.100) | data formatting | bytes 12288

commit v4 on v3

--- a/solution.py
+++ b/solution.py
@@ -78,7 +78,7 @@
     sizes,
     pos_ref, feat_ref, f1_ref, f2_ref, rin_ref, rout_ref, cw_ref, wave_ref, nb_ref, live_ref,
     out_ref,
-    wide, zwide, post, xpad, own_t, nf, wtab, thi, tlo, vhi, vlo, ahi, alo, uhi, ulo, zf, zz, geo,
+    wide, zwide, post, xpad, own_t, nf, wtab, tab, vmat, amat, umat, zf, zz, geo,
     wd1, wd2, wcol1, wcol2, gwt, gw, buf_a, buf_b, qsum, tslot, tsend, trecv, qbuf, sfb, rsb, agb, agpart, rmat,
     cgs, cgr, wf, pg, fsend, frecv, inv,
     ssem, rsem, halo_r, group_r, greet_sem,
@@ -192,13 +192,14 @@
                 col = post[block, pl.ds(at, rows_t), a : a + 1] * (1.0 / sides[a])
                 cols.append(col - jnp.round(col))
             row = pl.ds(pl.multiple_of(block * bs + at, rows_t), rows_t)
+            low_row = pl.ds(pl.multiple_of((n_blk + block) * bs + at, rows_t), rows_t)
             for start in range(0, n_wave, span):
                 lanes = slice(start, start + span)
                 u = cols[0] * nf[0:1, lanes] + cols[1] * nf[1:2, lanes] + cols[2] * nf[2:3, lanes]
                 sine, cosine = sin_cos_turns(u - jnp.round(u))
-                thi[row, lanes], tlo[row, lanes] = split(cosine)
+                tab[row, lanes], tab[low_row, lanes] = split(cosine)
                 later = slice(n_wave + start, n_wave + start + span)
-                thi[row, later], tlo[row, later] = split(sine)
+                tab[row, later], tab[low_row, later] = split(sine)
             return carry
 
         lax.fori_loop(0, bs // rows_t, one, 0)
@@ -235,7 +236,7 @@
         cosine = cosine * active
         return active, inverse, rho, bell, tau, tin, sine, cosine, cosine * cosine
 
-    def upright_pairs(s, block):
+    def upright_pairs(s, block, high_at, low_at):
         lanes = pl.ds(pl.multiple_of(s * bs, bs), bs)
         alive = jnp.where(s < live, 1.0, 0.0).astype(f32)
         put_values(zf, wide[block, 0:n_f, :], lanes)
@@ -247,20 +248,21 @@
             shaped = shape(dx, dy, dz, start, s, alive)
             bell, tau, tin, cut = shaped[3], shaped[4], shaped[5], shaped[8]
             first = cut * bell
-            out = pl.ds(pl.multiple_of(s * bs + start, rows_g), rows_g)
+            out = pl.ds(pl.multiple_of(high_at + start, rows_g), rows_g)
+            low_out = pl.ds(pl.multiple_of(low_at + start, rows_g), rows_g)
             term = first
             for m in range(half_m, n_m):
                 place = slice(m * bs, (m + 1) * bs)
-                uhi[out, place], ulo[out, place] = split(term)
+                umat[out, place], umat[low_out, place] = split(term)
                 term = term * tau
             term = first
             for m in range(half_m - 1, -1, -1):
                 term = term * tin
                 place = slice(m * bs, (m + 1) * bs)
-                uhi[out, place], ulo[out, place] = split(term)
+                umat[out, place], umat[low_out, place] = split(term)
 
     def near_upright(s, carry):
-        upright_pairs(s, near_id(s))
+        upright_pairs(s, near_id(s), (s + 1) * bs, (s + n_slot) * bs)
         return carry
 
     def pairs(s, block):
@@ -283,13 +285,15 @@
             term = first
             for m in range(half_m, n_m):
                 out = slice(m * bs + start, m * bs + start + rows_g)
-                ahi[out, lanes], alo[out, lanes] = split(term)
+                low_out = slice(out.start + n_m * bs, out.stop + n_m * bs)
+                amat[out, lanes], amat[low_out, lanes] = split(term)
                 term = term * tau
             term = first
             for m in range(half_m - 1, -1, -1):
                 term = term * tin
                 out = slice(m * bs + start, m * bs + start + rows_g)
-                ahi[out, lanes], alo[out, lanes] = split(term)
+                low_out = slice(out.start + n_m * bs, out.stop + n_m * bs)
+                amat[out, lanes], amat[low_out, lanes] = split(term)
 
     def near_pairs(s, carry):
         pairs(s, near_id(s))
@@ -299,9 +303,10 @@
 
     def messages(values, wcol, lanes, total):
         stack = values[0 : 2 * n_f, lanes]
+        stack = jnp.concatenate([stack, stack], axis=1)
         for g in range(0, n_m, group):
             place = slice(g * bs, (g + group) * bs)
-            got = dot_nn(stack, uhi[lanes, place]) + dot_nn(stack, ulo[lanes, place])
+            got = dot_nn(stack, umat[2 * lanes.start : 2 * lanes.stop, place])
             got = got[0:n_f] + got[n_f:]
             for m in range(group):
                 weights = wcol[0:n_f, g + m : g + m + 1]
@@ -315,7 +320,7 @@
             values[:, spare] = jnp.zeros((4 * n_f, wide_p - wide_n), bf16)
         for index in range(3, 7):
             geo[index, :, spare] = jnp.zeros((bs, wide_p - wide_n), f32)
-    upright_pairs(0, mine)
+    upright_pairs(0, mine, 0, bs)
     total = messages(zf, wcol1, first_lanes, wide[mine, 0:n_f, :])
     met(1, rounds[0])
     greet(2, rounds[1])
@@ -347,20 +352,44 @@
     gate = 1.0 / (1.0 + jnp.exp(-hidden))
     bent = gate * (1.0 + hidden * (1.0 - gate))
     short_grad = exact_nn(rin_ref[...] * rout_ref[...], bent)
-    wait_bytes(qbuf.at[pl.ds(0, n_k - 1)], rsem.at[2])
-
-    charges = jnp.concatenate([qbuf[c] for c in range(n_blk)], axis=1)
-    stacked = jnp.concatenate(split(charges), axis=0)
-    met(4, rounds[3])
+
     pair_k = n_group // 2
     span_k = pair_k * bs
     groups = n_at // n_group
+    places = []
+    for a in range(3):
+        turns = pos_ref[a : a + 1, :] * (1.0 / sides[a])
+        places.append(turns - jnp.round(turns))
+
+    def upright_tables(chunk, carry):
+        down = nf[:, pl.ds(pl.multiple_of(chunk * bs, bs), bs)].T
+        at = (chunk // pair_k) * (4 * span_k) + lax.rem(chunk, pair_k) * bs
+        for start in range(0, bs, rows_t):
+            ks = [down[start : start + rows_t, a : a + 1] for a in range(3)]
+            u = ks[0] * places[0] + ks[1] * places[1] + ks[2] * places[2]
+            sine, cosine = sin_cos_turns(u - jnp.round(u))
+            rows = [
+                pl.ds(pl.multiple_of(at + part * span_k + start, rows_t), rows_t)
+                for part in range(4)
+            ]
+            vmat[rows[0], :], vmat[rows[2], :] = split(cosine)
+            vmat[rows[1], :], vmat[rows[3], :] = split(sine)
+        return carry
+
+    q_chunks, rs_chunks = k_chunks * 7 // 16, k_chunks * 10 // 16
+    lax.fori_loop(0, q_chunks, upright_tables, 0)
+    wait_bytes(qbuf.at[pl.ds(0, n_k - 1)], rsem.at[2])
+
+    charges = jnp.concatenate([qbuf[c] for c in range(n_blk)], axis=1)
+    stacked = jnp.concatenate(split(charges), axis=0)
+    stacked = jnp.concatenate([stacked, stacked], axis=1)
+    met(4, rounds[3])
     own_group, own_place = p // n_group, lax.rem(p, n_group)
     for step in range(groups):
         this = lax.rem(own_group + step, groups)
         for kind in range(2):
             lanes = pl.ds(pl.multiple_of(kind * n_wave + this * span_k, bs), span_k)
-            got = dot_nn(stacked, thi[:, lanes]) + dot_nn(stacked, tlo[:, lanes])
+            got = dot_nn(stacked, tab[:, lanes])
             got = got[0:n_q] + got[n_q:]
             for c in range(pair_k):
                 sfb[this * n_group + 2 * c + kind] = got[:, c * bs : (c + 1) * bs]
@@ -371,6 +400,7 @@
             send(sfb.at[target], rsb.at[ahead - 1], 3, ahead, 0)
     pairs(0, mine)
     lax.fori_loop(1, n_slot, near_pairs, 0)
+    lax.fori_loop(q_chunks, rs_chunks, upright_tables, 0)
     wait_bytes(rsb, rsem.at[3])
     part = sfb[p]
     for d in range(n_at - 1):
@@ -382,25 +412,7 @@
     keep = pltpu.make_async_copy(agpart, agb.at[p], group_r.at[own_group])
     keep.start()
 
-    places = []
-    for a in range(3):
-        turns = pos_ref[a : a + 1, :] * (1.0 / sides[a])
-        places.append(turns - jnp.round(turns))
-
-    def upright_tables(chunk, carry):
-        at = pl.multiple_of(chunk * bs, bs)
-        down = nf[:, pl.ds(at, bs)].T
-        for start in range(0, bs, rows_t):
-            ks = [down[start : start + rows_t, a : a + 1] for a in range(3)]
-            u = ks[0] * places[0] + ks[1] * places[1] + ks[2] * places[2]
-            sine, cosine = sin_cos_turns(u - jnp.round(u))
-            row = pl.ds(pl.multiple_of(at + start, rows_t), rows_t)
-            vhi[row, :], vlo[row, :] = split(cosine)
-            row = pl.ds(pl.multiple_of(n_wave + at + start, rows_t), rows_t)
-            vhi[row, :], vlo[row, :] = split(sine)
-        return carry
-
-    lax.fori_loop(0, k_chunks, upright_tables, 0)
+    lax.fori_loop(rs_chunks, k_chunks, upright_tables, 0)
 
     total = jnp.zeros((8 * n_q, n_blk * bs), f32)
     for step in range(groups):
@@ -415,14 +427,12 @@
             rows2 = [sin_part] + [cos_part * -k for k in ks]
             for kind, pieces in ((0, rows), (1, rows2)):
                 place = slice(kind * span_k + c * bs, kind * span_k + (c + 1) * bs)
-                for a, piece in enumerate(pieces):
-                    high, low = split(piece)
-                    rmat[step, a * n_q : (a + 1) * n_q, place] = high
-                    rmat[step, (4 + a) * n_q : (5 + a) * n_q, place] = low
-        for kind in range(2):
-            lanes = pl.ds(pl.multiple_of(kind * n_wave + this * span_k, bs), span_k)
-            right = rmat[step, :, kind * span_k : (kind + 1) * span_k]
-            total = total + dot_nn(right, vhi[lanes, :]) + dot_nn(right, vlo[lanes, :])
+                high, low = split(jnp.concatenate(pieces, axis=0))
+                rmat[step, 0 : 4 * n_q, place] = high
+                rmat[step, 4 * n_q :, place] = low
+        right = rmat[step]
+        rows = pl.ds(pl.multiple_of(this * (4 * span_k), 4 * span_k), 4 * span_k)
+        total = total + dot_nn(jnp.concatenate([right, right], axis=1), vmat[rows, :])
     total = total[0 : 4 * n_q] + total[4 * n_q :]
     folded = []
     for c in range(n_blk):
@@ -446,7 +456,8 @@
         high, low = split(g_two * wcol2[0:n_f, m : m + 1])
         gwt[0:n_f, lanes] = high
         gwt[n_f:, lanes] = low
-    got = dot_nn(gwt[...], ahi[...]) + dot_nn(gwt[...], alo[...])
+    twin = gwt[...]
+    got = dot_nn(jnp.concatenate([twin, twin], axis=1), amat[...])
     got = got[0:n_f] + got[n_f:]
     for s in range(n_slot):
         tslot[s] = got[:, s * bs : (s + 1) * bs]
@@ -595,14 +606,10 @@
         v((bs, bs), f32),
         v((8, n_wave), f32),
         v((k_chunks, 8, bs), f32),
-        v((local, 2 * n_wave), bf16),
-        v((local, 2 * n_wave), bf16),
-        v((2 * n_wave, local), bf16),
-        v((2 * n_wave, local), bf16),
-        v((n_m * bs, wide_n), bf16),
-        v((n_m * bs, wide_n), bf16),
-        v((wide_n, n_m * bs), bf16),
-        v((wide_n, n_m * bs), bf16),
+        v((2 * local, 2 * n_wave), bf16),
+        v((4 * n_wave, local), bf16),
+        v((2 * n_m * bs, wide_n), bf16),
+        v((2 * wide_n, n_m * bs), bf16),
         v((4 * n_f, wide_p), bf16),
         v((4 * n_f, wide_p), bf16),
         v((7, bs, wide_p), f32),

time: 67.3 us -> 66.4 us (0.987)
  Pallas kernels: 65.8 us -> 64.9 us
    pallas_call x1, Pallas kernels: 65.8 us -> 64.9 us  [body(): pl.pallas_call(functools.partial(kernel, sizes), out_shape=jax.ShapeDtype...]
where the time goes in v4:
time: 66.4 us; the launch traced here: 66.2 us
  Pallas kernels  64.9 us (98%)
  local copies, waits for them, and re-layouts  1.3 us (2%)
    pallas_call x1, Pallas kernels, body(): pl.pallas_call(functools.partial(kernel, sizes), out_shape=jax.ShapeDtype...  64.9 us

profile of v4, /device:TPU:0, one launch (start us, length us, event | category | flops | bytes accessed | tf_op | source)
XLA Modules:
  0.0 66.2 jit_solution(1297573523556654482)
XLA Ops:
  0.0 64.9 %shard_map.100 = f32[3,512]{1,0:T(4,128)} custom-call(f32[3,512]{1,0:T(4,128)} %pos_ref.1, f32[64,512]{1,0:T(8,128)} %feat_ref.1, f32[16,64]{1,0:T(8,128)} %f1_ref.1, f32[16,64]{1,0:T(8,128)} %f2_ref.1, f32[64,64]{1,0:T(8,128)} %rin_ref.1, f32[1,64]{1,0:T(1,128)} %bitcast.3, f32[16,64]{1,0:T(8,128)} %bitcast.2, s32[3,2048]{1,0:T(4,128)} %wave_ref.1, ...), custom_call_target="tpu_custom_call" | custom-call | tf_op jit(solution)/shard_map/pallas_call | solution.py:649
  65.0 1.3 %copy.12 = f32[3,512]{1,0:T(4,128)} copy(f32[3,512]{1,0:T(4,128)} %shard_map.100) | data formatting | bytes 12288

commit v5 on v4

--- a/solution.py
+++ b/solution.py
@@ -89,7 +89,6 @@
     q = lax.axis_index("kvec")
     half_m = n_m // 2
     wide_n = n_slot * bs
-    wide_p = zf.shape[1]
     k_chunks = n_wave // bs
     across = [(0, dq) for dq in range(1, n_k)]
     beside = [(1, 0), (-1, 0)]
@@ -314,12 +313,6 @@
         return total
 
     first_lanes, later_lanes = slice(0, bs), slice(bs, wide_n)
-    if wide_p > wide_n:
-        spare = slice(wide_n, wide_p)
-        for values in (zf, zz):
-            values[:, spare] = jnp.zeros((4 * n_f, wide_p - wide_n), bf16)
-        for index in range(3, 7):
-            geo[index, :, spare] = jnp.zeros((bs, wide_p - wide_n), f32)
     upright_pairs(0, mine, 0, bs)
     total = messages(zf, wcol1, first_lanes, wide[mine, 0:n_f, :])
     met(1, rounds[0])
@@ -467,11 +460,9 @@
         tsend[index] = tslot[inv[block]]
         send(tsend.at[index], trecv.at[index], 6, dp, dq)
 
-    rows_c = 32
-    rows_h = 16
-    tile = 2 * bs
-    tiles = wide_p // tile
-    steps_p = bs // rows_c * tiles
+    rows_c = 16
+    steps_p = bs // rows_c
+    width = 3 * bs
 
     def pair_sums(grad, wd, values, last):
         twice = jnp.concatenate([grad, grad], axis=0).T
@@ -485,17 +476,16 @@
 
         def product(step, buf):
             height = n_m * rows_c
-            rows = pl.ds(pl.multiple_of(step // tiles * height, height), height)
-            lanes = pl.ds(pl.multiple_of(lax.rem(step, tiles) * tile, tile), tile)
-            buf[...] = dot_nn(gw[rows, :], values[:, lanes])
+            rows = pl.ds(pl.multiple_of(step * height, height), height)
+            buf[...] = dot_nn(gw[rows, :], values[...])
 
         def horner(step, buf):
-            lanes = pl.ds(pl.multiple_of(lax.rem(step, tiles) * tile, tile), tile)
-            for part in range(0, rows_c, rows_h):
-                rows = pl.ds(pl.multiple_of(step // tiles * rows_c + part, rows_h), rows_h)
+            rows = pl.ds(pl.multiple_of(step * rows_c, rows_c), rows_c)
+            for start in range(0, wide_n, width):
+                lanes = slice(start, min(start + width, wide_n))
 
                 def term(m):
-                    return buf[m * rows_c + part : m * rows_c + part + rows_h, :]
+                    return buf[m * rows_c : (m + 1) * rows_c, lanes]
 
                 tau = geo[3, rows, lanes]
                 tin = geo[4, rows, lanes]
@@ -593,7 +583,6 @@
     n_wave = wave_ints.shape[1]
     local = n_blk * bs
     wide_n = n_slot * bs
-    wide_p = (n_slot + n_slot % 2) * bs
     near_n = 3 * n_blk - 1
     k_chunks = n_wave // bs
     sizes = (n_at, n_k, n_blk, bs, n_slot, n_f, n_m, n_q, n_wave)
@@ -610,18 +599,18 @@
         v((4 * n_wave, local), bf16),
         v((2 * n_m * bs, wide_n), bf16),
         v((2 * wide_n, n_m * bs), bf16),
-        v((4 * n_f, wide_p), bf16),
-        v((4 * n_f, wide_p), bf16),
-        v((7, bs, wide_p), f32),
+        v((4 * n_f, wide_n), bf16),
+        v((4 * n_f, wide_n), bf16),
+        v((7, bs, wide_n), f32),
         v((n_m, 2 * n_f), f32),
         v((n_m, 2 * n_f), f32),
         v((bs, bs), f32),
         v((bs, bs), f32),
         v((2 * n_f, n_m * bs), bf16),
         v((n_m * bs, 4 * n_f), bf16),
-        v((n_m * 32, 2 * bs), f32),
-        v((n_m * 32, 2 * bs), f32),
-        v((bs, wide_p), f32),
+        v((n_m * 16, wide_n), f32),
+        v((n_m * 16, wide_n), f32),
+        v((bs, wide_n), f32),
         v((n_slot + 1, n_f, bs), f32),
         v((near_n, n_f, bs), f32),
         v((near_n, n_f, bs), f32),

time: 66.4 us -> 65.2 us (0.982)
  Pallas kernels: 64.9 us -> 63.7 us
    pallas_call x1, Pallas kernels: 64.9 us -> 63.7 us  [body(): pl.pallas_call(functools.partial(kernel, sizes), out_shape=jax.ShapeDtype...]
where the time goes in v5:
time: 65.2 us; the launch traced here: 65.1 us
  Pallas kernels  63.7 us (98%)
  local copies, waits for them, and re-layouts  1.3 us (2%)
    pallas_call x1, Pallas kernels, body(): pl.pallas_call(functools.partial(kernel, sizes), out_shape=jax.ShapeDtype...  63.7 us

profile of v5, /device:TPU:0, one launch (start us, length us, event | category | flops | bytes accessed | tf_op | source)
XLA Modules:
  0.0 65.1 jit_solution(6301012851356806457)
XLA Ops:
  0.0 63.7 %shard_map.100 = f32[3,512]{1,0:T(4,128)} custom-call(f32[3,512]{1,0:T(4,128)} %pos_ref.1, f32[64,512]{1,0:T(8,128)} %feat_ref.1, f32[16,64]{1,0:T(8,128)} %f1_ref.1, f32[16,64]{1,0:T(8,128)} %f2_ref.1, f32[64,64]{1,0:T(8,128)} %rin_ref.1, f32[1,64]{1,0:T(1,128)} %bitcast.3, f32[16,64]{1,0:T(8,128)} %bitcast.2, s32[3,2048]{1,0:T(4,128)} %wave_ref.1, ...), custom_call_target="tpu_custom_call" | custom-call | tf_op jit(solution)/shard_map/pallas_call | solution.py:638
  63.8 1.3 %copy.12 = f32[3,512]{1,0:T(4,128)} copy(f32[3,512]{1,0:T(4,128)} %shard_map.100) | data formatting | bytes 12288

commit v6 on v5

--- a/solution.py
+++ b/solution.py
@@ -460,9 +460,9 @@
         tsend[index] = tslot[inv[block]]
         send(tsend.at[index], trecv.at[index], 6, dp, dq)
 
-    rows_c = 16
+    rows_c = 32
     steps_p = bs // rows_c
-    width = 3 * bs
+    width = bs
 
     def pair_sums(grad, wd, values, last):
         twice = jnp.concatenate([grad, grad], axis=0).T
@@ -608,8 +608,8 @@
         v((bs, bs), f32),
         v((2 * n_f, n_m * bs), bf16),
         v((n_m * bs, 4 * n_f), bf16),
-        v((n_m * 16, wide_n), f32),
-        v((n_m * 16, wide_n), f32),
+        v((n_m * 32, wide_n), f32),
+        v((n_m * 32, wide_n), f32),
         v((bs, wide_n), f32),
         v((n_slot + 1, n_f, bs), f32),
         v((near_n, n_f, bs), f32),

time: 65.2 us -> 64.7 us (level)
  no operation moved by 1% of the time
where the time goes in v6:
time: 64.7 us; the launch traced here: 64.6 us
  Pallas kernels  63.3 us (98%)
  local copies, waits for them, and re-layouts  1.3 us (2%)
    pallas_call x1, Pallas kernels, body(): pl.pallas_call(functools.partial(kernel, sizes), out_shape=jax.ShapeDtype...  63.3 us
    unnamed x1, local copies, waits for them, and re-layouts  1.3 us

profile of v6, /device:TPU:0, one launch (start us, length us, event | category | flops | bytes accessed | tf_op | source)
XLA Modules:
  0.0 64.6 jit_solution(9833820095922198305)
XLA Ops:
  0.0 63.3 %shard_map.100 = f32[3,512]{1,0:T(4,128)} custom-call(f32[3,512]{1,0:T(4,128)} %pos_ref.1, f32[64,512]{1,0:T(8,128)} %feat_ref.1, f32[16,64]{1,0:T(8,128)} %f1_ref.1, f32[16,64]{1,0:T(8,128)} %f2_ref.1, f32[64,64]{1,0:T(8,128)} %rin_ref.1, f32[1,64]{1,0:T(1,128)} %bitcast.3, f32[16,64]{1,0:T(8,128)} %bitcast.2, s32[3,2048]{1,0:T(4,128)} %wave_ref.1, ...), custom_call_target="tpu_custom_call" | custom-call | tf_op jit(solution)/shard_map/pallas_call | solution.py:638
  63.3 1.3 %copy.12 = f32[3,512]{1,0:T(4,128)} copy(f32[3,512]{1,0:T(4,128)} %shard_map.100) | data formatting | bytes 12288
